TPU v7x, 256 devices: a whole 4x4x8 slice. The times are simulated.
256 devices in a mesh: pts: 64 (over z, y, core), rep: 4 (over x).
Axes of the slice: x: 4, y: 4, z: 8, core: 2. Of those that a mesh axis runs over, the one named last changes fastest.
Arguments:
- feats: bfloat16 [4, 131072, 64], P('rep', 'pts'), may hold values from -6 to 6
- dest_first: int32 [4, 131072], P('rep', 'pts'), may hold values from 0 to 131071, as said below
- pool_ids: int32 [4, 131072], P('rep', 'pts'), may hold values from 0 to 511, as said below
- dest_second: int32 [4, 32768], P('rep', 'pts'), may hold values from 0 to 32767, as said below
- cotangent: bfloat16 [4, 32768, 128], P('rep', 'pts'), may hold values from -6 to 6
- inlet_first: bfloat16 [64, 192], replicated, may hold values from -0.75 to 0.75
- outlet_first: bfloat16 [64, 64], replicated, may hold values from -0.75 to 0.75
- widen_first: bfloat16 [64, 256], replicated, may hold values from -0.75 to 0.75
- narrow_first: bfloat16 [256, 64], replicated, may hold values from -0.375 to 0.375
- pool_weight: bfloat16 [64, 128], replicated, may hold values from -0.75 to 0.75
- inlet_second: bfloat16 [128, 384], replicated, may hold values from -0.5 to 0.5
- outlet_second: bfloat16 [128, 128], replicated, may hold values from -0.5 to 0.5
- widen_second: bfloat16 [128, 512], replicated, may hold values from -0.5 to 0.5
- narrow_second: bfloat16 [512, 128], replicated, may hold values from -0.25 to 0.25
Outputs:
- second_out: bfloat16 [4, 32768, 128], P('rep', 'pts')
- feats_grad: bfloat16 [4, 131072, 64], P('rep', 'pts')
- grad_inlet_first: float32 [64, 192], replicated
- grad_outlet_first: float32 [64, 64], replicated
- grad_widen_first: float32 [64, 256], replicated
- grad_narrow_first: float32 [256, 64], replicated
- grad_pool_weight: float32 [64, 128], replicated
- grad_inlet_second: float32 [128, 384], replicated
- grad_outlet_second: float32 [128, 128], replicated
- grad_widen_second: float32 [128, 512], replicated
- grad_narrow_second: float32 [512, 128], replicated
Inputs may be any that keep to these rules, and one draw needn't show every extreme that they name: For each scan a permutation of the positions; the points of one device (aligned blocks of 2048) go to device dest_first // 2048 with at most 64 of them to any one device, and exactly 64 to some devices. `pool_ids`: within each aligned block of 2048 rows the values never fall, every value from 0 to 511 occurs on 1 to 7 consecutive rows, and some value on exactly 7. For each scan a permutation of the positions; the pooled points of one device (aligned blocks of 512) go to device dest_second // 512 with at most 16 of them to any one device, and exactly 16 to some devices.
All inputs are finite; a program needn't handle non-finite values.
Results may differ from a plain program's by a relative error of at most 0.028.
Values may be sent and summed in bfloat16 or wider, within the bound.
A program may use at most 128 MiB of HBM per device.

v0:
```python
import math

import jax
import jax.numpy as jnp
from jax import lax
from jax.sharding import PartitionSpec as P

HEAD_SIZE = 16
PATCH = 512


def shortened(array):

    def short(part):
        return part.astype(jnp.bfloat16) if part.dtype == jnp.float32 else part

    return jax.tree.map(short, array)


def layer_norm(values):
    centred = values - jnp.mean(values, axis=-1, keepdims=True)
    return centred * lax.rsqrt(jnp.mean(centred * centred, axis=-1, keepdims=True) + 1e-05)


def zero_taps(row_count, feature_width):
    return (
        jnp.zeros((row_count, 3 * feature_width), jnp.float32),
        jnp.zeros((row_count, feature_width), jnp.float32),
        jnp.zeros((row_count, 4 * feature_width), jnp.float32),
        jnp.zeros((row_count, feature_width), jnp.float32),
    )


def block(inputs, weights, tap_zeros):
    inlet_weight, outlet, widen_weight, narrow = weights
    row_count, feature_width = inputs.shape
    head_count = feature_width // HEAD_SIZE
    initial = inputs.astype(jnp.float32)
    normed = layer_norm(initial).astype(jnp.bfloat16)
    mixed_rows = (
        jnp.dot(normed, inlet_weight, preferred_element_type=jnp.float32) + tap_zeros[0]
    ).astype(jnp.bfloat16)
    parted = mixed_rows.reshape(row_count // PATCH, PATCH, 3, head_count, HEAD_SIZE)
    scores = jnp.einsum(
        "bqhd,bkhd->bhqk", parted[:, :, 0], parted[:, :, 1], preferred_element_type=jnp.float32
    ) * HEAD_SIZE ** (-0.5)
    softmax_weights = jax.nn.softmax(scores, axis=-1).astype(jnp.bfloat16)
    attended = jnp.einsum(
        "bhqk,bkhd->bqhd", softmax_weights, parted[:, :, 2], preferred_element_type=jnp.float32
    )
    attended = attended.astype(jnp.bfloat16).reshape(row_count, feature_width)
    middle = initial + jnp.dot(attended, outlet, preferred_element_type=jnp.float32) + tap_zeros[1]
    second = layer_norm(middle).astype(jnp.bfloat16)
    hidden = jax.nn.gelu(
        jnp.dot(second, widen_weight, preferred_element_type=jnp.float32) + tap_zeros[2],
        approximate=False,
    ).astype(jnp.bfloat16)
    result = (
        middle + jnp.dot(hidden, narrow, preferred_element_type=jnp.float32) + tap_zeros[3]
    ).astype(jnp.bfloat16)
    return (result, (normed, attended, second, hidden))


def weight_grad(inputs, gradient):
    return lax.dot_general(
        inputs,
        gradient.astype(jnp.bfloat16),
        (((0,), (0,)), ((), ())),
        preferred_element_type=jnp.float32,
    )


def run_block(inputs, weights):
    tap_zeros = zero_taps(inputs.shape[0], inputs.shape[1])
    result, pullback, saved = jax.vjp(
        lambda given, taps_in: block(given, weights, taps_in), inputs, tap_zeros, has_aux=True
    )

    def finish(gradient):
        grad_rows, grad_taps = pullback(gradient)
        return (
            grad_rows,
            tuple((weight_grad(saved[index], grad_taps[index]) for index in range(4))),
        )

    return (result, finish)


def pool_rows(inputs, ident, coarse_count):
    member = ident[None, :] == jnp.arange(coarse_count, dtype=jnp.int32)[:, None]
    sums = jnp.dot(member.astype(jnp.bfloat16), inputs, preferred_element_type=jnp.float32)
    sizes = jnp.sum(member.astype(jnp.float32), axis=1, keepdims=True)
    return (sums / sizes).astype(jnp.bfloat16)


def project(pooled, weight, tap_zero):
    return (jnp.dot(pooled, weight, preferred_element_type=jnp.float32) + tap_zero).astype(
        jnp.bfloat16
    )


def run_project(pooled, weight):
    tap_zero = jnp.zeros((pooled.shape[0], weight.shape[1]), jnp.float32)
    result, pullback = jax.vjp(
        lambda given, tap_in: project(given, weight, tap_in), pooled, tap_zero
    )

    def finish(gradient):
        grad_pooled, grad_tap = pullback(gradient)
        return (grad_pooled, weight_grad(pooled, grad_tap))

    return (result, finish)


def pack_slots(targets, row_count, devices, capacity):
    owner = targets // row_count
    place_index = targets % row_count
    hits = (owner[:, None] == jnp.arange(devices, dtype=jnp.int32)[None, :]).astype(jnp.int32)
    rank = jnp.sum(hits * (jnp.cumsum(hits, axis=0) - 1), axis=1)
    slot_index = owner * capacity + rank
    landing = jnp.full((devices * capacity,), row_count, jnp.int32).at[slot_index].set(place_index)
    return (slot_index, landing.reshape(devices, capacity))


def fill_slots(inputs, slot_index, devices, capacity):
    buffer = (
        jnp.zeros((devices * capacity, inputs.shape[1]), inputs.dtype).at[slot_index].set(inputs)
    )
    return buffer.reshape(devices, capacity, inputs.shape[1])


def land_rows(arrived, landing, row_count):
    feature_width = arrived.shape[2]
    placed = (
        jnp.zeros((row_count + 1, feature_width), arrived.dtype)
        .at[landing.reshape(-1)]
        .set(arrived.reshape(-1, feature_width))
    )
    return placed[:row_count]


def take_rows(gradient, landing, devices, capacity):
    feature_width = gradient.shape[1]
    padded = jnp.concatenate([gradient, jnp.zeros((1, feature_width), gradient.dtype)], axis=0)
    return padded[landing.reshape(-1)].reshape(devices, capacity, feature_width)


def pick_rows(returned, slot_index):
    return returned.reshape(-1, returned.shape[2])[slot_index]


def shards(
    feats,
    dest_first,
    pool_ids,
    dest_second,
    cotangent,
    inlet_first,
    outlet_first,
    widen_first,
    narrow_first,
    pool_weight,
    inlet_second,
    outlet_second,
    widen_second,
    narrow_second,
):
    first = (inlet_first, outlet_first, widen_first, narrow_first)
    second = (inlet_second, outlet_second, widen_second, narrow_second)
    devices = lax.axis_size("pts")
    point_rows = feats[0]
    row_count, width_one = point_rows.shape
    coarse_count = dest_second.shape[1]
    capacity_one = 2 * row_count // devices
    capacity_two = 2 * coarse_count // devices
    slot_one, landing_one = pack_slots(dest_first[0], row_count, devices, capacity_one)
    sent_rows, arrived_one = (
        lax.all_to_all(
            fill_slots(point_rows, slot_one, devices, capacity_one),
            "pts",
            split_axis=0,
            concat_axis=0,
            tiled=True,
        ),
        lax.all_to_all(landing_one, "pts", split_axis=0, concat_axis=0, tiled=True),
    )
    serial_one = land_rows(sent_rows, arrived_one, row_count)
    ident = pool_ids[0]
    fine_out, finish_first = run_block(serial_one, first)
    pooled, finish_pool = jax.vjp(lambda given: pool_rows(given, ident, coarse_count), fine_out)
    slot_two, landing_two = pack_slots(dest_second[0], coarse_count, devices, capacity_two)
    coarse_in, finish_proj = run_project(pooled, pool_weight)
    moved, arrived_two = (
        lax.all_to_all(
            shortened(fill_slots(coarse_in, slot_two, devices, capacity_two)),
            "pts",
            split_axis=0,
            concat_axis=0,
            tiled=True,
        ),
        lax.all_to_all(landing_two, "pts", split_axis=0, concat_axis=0, tiled=True),
    )
    serial_two = land_rows(moved, arrived_two, coarse_count)
    second_out, finish_second = run_block(serial_two, second)
    grad_serial_two, grads_second = finish_second(cotangent[0])
    returned = lax.all_to_all(
        shortened(take_rows(grad_serial_two, arrived_two, devices, capacity_two)),
        "pts",
        split_axis=0,
        concat_axis=0,
        tiled=True,
    )
    grad_pooled, grad_pool = finish_proj(pick_rows(returned, slot_two))
    grad_fine = finish_pool(grad_pooled)[0]
    grad_serial_one, grads_first = finish_first(grad_fine)
    back_rows = lax.all_to_all(
        shortened(take_rows(grad_serial_one, arrived_one, devices, capacity_one)),
        "pts",
        split_axis=0,
        concat_axis=0,
        tiled=True,
    )
    feats_grad = pick_rows(back_rows, slot_one)
    totals = lax.psum(
        (
            grads_first[0],
            grads_first[1],
            grads_first[2],
            grads_first[3],
            grad_pool,
            grads_second[0],
            grads_second[1],
            grads_second[2],
            grads_second[3],
        ),
        ("pts", "rep"),
    )
    scale = 1.0 / math.sqrt(lax.axis_size("rep") * devices * coarse_count)
    scaled = tuple((total * scale for total in totals))
    return (
        second_out[None],
        feats_grad[None],
        scaled[0],
        scaled[1],
        scaled[2],
        scaled[3],
        scaled[4],
        scaled[5],
        scaled[6],
        scaled[7],
        scaled[8],
    )


def solution(mesh):
    return jax.shard_map(
        shards,
        mesh=mesh,
        in_specs=(
            P("rep", "pts", None),
            P("rep", "pts"),
            P("rep", "pts"),
            P("rep", "pts"),
            P("rep", "pts", None),
            P(),
            P(),
            P(),
            P(),
            P(),
            P(),
            P(),
            P(),
            P(),
        ),
        out_specs=(
            P("rep", "pts", None),
            P("rep", "pts", None),
            P(),
            P(),
            P(),
            P(),
            P(),
            P(),
            P(),
            P(),
            P(),
        ),
        check_vma=False,
    )
```

profile of v0, /device:TPU:32, one launch (start us, length us, event | category | flops | bytes accessed | tf_op | source)
XLA Modules:
  0.0 799.1 jit_solution(12828813853988882217)
XLA Ops:
  10.9 2.4 scatter_custom_fusion
  14.1 11.8 %all-to-all-start = ((s32[64,1,16]{2,1,0:T(1,128)}), s32[64,1,16]{2,1,0:T(1,128)S(1)}, u32[]{:S(2)}, u32[]{:S(2)}) async-start(s32[64,1,16]{2,1,0:T(1,128)} %bitcast.6), calls=%async_computation | async-start | bytes 65536 | tf_op jit(solution)/shard_map/all_to_all | solution.py:201
  26.6 18.1 %reduce-window.16 = s32[64,16,128]{2,1,0:T(8,128)S(1)} reduce-window(s32[64,16,128]{2,1,0:T(8,128)S(1)} %fusion.86, s32[]{:T(128)} %constant.59.clone.1), window={size=1x1x128 pad=0_0x0_0x127_0}, to_apply=%region_4.5 | reduce-window | flops 16646144 | bytes 1048580 | tf_op jit(solution)/shard_map/reduce-window.2
  47.2 8.1 %scatter_custom_fusion.1 = s32[4096]{0:T(1024)S(1)} fusion(s32[2048]{0:T(1024)S(1)} %bitcast.296, s32[2048]{0:T(1024)S(1)} %get-tuple-element.75, s32[]{:T(128)} %constant.66.clone.1), kind=kCustom, calls=%fused_computation.260 | custom fusion | bytes 16388 | tf_op jit(solution)/shard_map/scatter | solution.py:121
  56.0 10.3 %all-to-all-start.1 = ((s32[64,1,64]{2,1,0:T(1,128)}), s32[64,1,64]{2,1,0:T(1,128)S(1)}, u32[]{:S(2)}, u32[]{:S(2)}) async-start(s32[64,1,64]{2,1,0:T(1,128)} %all_to_all.26), calls=%async_computation.1 | async-start | bytes 65536 | tf_op jit(solution)/shard_map/all_to_all | solution.py:185
  67.2 6.1 scatter_custom_fusion.2
  76.1 10.3 %all-to-all-start.2 = ((bf16[64,2,2048]{2,1,0:T(2,128)(2,1)}), bf16[64,2,2048]{2,1,0:T(2,128)(2,1)S(1)}, u32[]{:S(2)}, u32[]{:S(2)}) async-start(bf16[64,2,2048]{2,1,0:T(2,128)(2,1)} %reshape.709), calls=%async_computation.2 | async-start | bytes 1048576 | tf_op jit(solution)/shard_map/all_to_all | solution.py:178
  87.3 15.9 %all-to-all-done.2 = bf16[64,2,2048]{2,1,0:T(2,128)(2,1)S(1)} async-done(((bf16[64,2,2048]{2,1,0:T(2,128)(2,1)}), bf16[64,2,2048]{2,1,0:T(2,128)(2,1)S(1)}, u32[]{:S(2)}, u32[]{:S(2)}) %all-to-all-start.2) | async-done | bytes 524320 | tf_op jit(solution)/shard_map/all_to_all | solution.py:178
  103.9 11.2 %scatter_custom_fusion.3 = bf16[2049,64]{1,0:T(8,128)(2,1)S(1)} fusion(s32[4096]{0:T(1024)S(1)} %bitcast.292, bf16[4096,64]{1,0:T(8,128)(2,1)S(1)} %bitcast.284, bf16[]{:T(256)} %constant.56.clone.1), kind=kCustom, calls=%fused_computation.176 | custom fusion | bytes 262274 | tf_op jit(solution)/shard_map/scatter | solution.py:137
  118.0 8.8 %fusion.153 = (f32[4,4,512]{2,1,0:T(4,128)S(1)}, f32[4,4,512,512]{2,3,1,0:T(8,128)}) fusion(bf16[4,512,1,4,16]{1,0,4,3,2:T(4,128)(2,1)S(1)} %get-tuple-element.73, bf16[4,512,1,4,16]{1,0,4,3,2:T(4,128)(2,1)S(1)} %get-tuple-element.74), kind=kOutput, calls=%fused_computation.312 | convolution fusion | flops 146801152 | bytes 17334272 | tf_op jit(solution)/shard_map/jvp()/sub | solution.py:47
  126.8 7.1 divide_convert_fusion
  137.9 6.2 multiply_convert_fusion
  145.6 2.6 scatter_custom_fusion.4
  148.1 15.8 %all-to-all-start.3 = ((bf16[64,16,128]{2,1,0:T(8,128)(2,1)}), bf16[64,16,128]{2,1,0:T(8,128)(2,1)S(1)}, u32[]{:S(2)}, u32[]{:S(2)}) async-start(bf16[64,16,128]{2,1,0:T(8,128)(2,1)} %bitcast.25), calls=%async_computation.3 | async-start | bytes 524288 | tf_op jit(solution)/shard_map/all_to_all | solution.py:194
  165.2 10.8 %all-to-all-done.3 = bf16[64,16,128]{2,1,0:T(8,128)(2,1)S(1)} async-done(((bf16[64,16,128]{2,1,0:T(8,128)(2,1)}), bf16[64,16,128]{2,1,0:T(8,128)(2,1)S(1)}, u32[]{:S(2)}, u32[]{:S(2)}) %all-to-all-start.3) | async-done | bytes 262176 | tf_op jit(solution)/shard_map/all_to_all | solution.py:194
  176.0 3.2 scatter_custom_fusion.5
  180.0 5.0 fusion.155
  185.0 4.6 divide_convert_fusion.1
  200.6 2.7 fusion.51
  205.8 4.6 gather_fusion
  210.5 5.9 all-to-all-start.4
  220.5 8.0 %all-to-all-done.4 = bf16[64,16,128]{2,1,0:T(8,128)(2,1)S(1)} async-done(((bf16[64,16,128]{2,1,0:T(8,128)(2,1)}), bf16[64,16,128]{2,1,0:T(8,128)(2,1)S(1)}, u32[]{:S(2)}, u32[]{:S(2)}) %all-to-all-start.4) | async-done | bytes 262176 | tf_op jit(solution)/shard_map/all_to_all | solution.py:206
  231.6 3.2 fusion.32
  237.7 5.7 fusion.43
  243.3 9.4 %fusion.6 = (f32[4,4,512]{2,1,0:T(4,128)S(1)}, bf16[4,4,512,512]{2,3,1,0:T(8,128)(2,1)}) fusion(f32[4,4,512,512]{2,3,1,0:T(8,128)} %get-tuple-element.80, f32[4,4,512]{2,1,0:T(4,128)S(1)} %multiply_divide_fusion, bf16[4,512,1,4,16]{1,0,4,3,2:T(4,128)(2,1)S(1)} %get-tuple-element.72, bf16[4,512,4,16]{1,0,3,2:T(4,128)(2,1)S(1)} %reshape.596), kind=kOutput, calls=%fused_computation.18 | convolution fusion | flops 155181056 | bytes 25755648 | tf_op jit(solution)/shard_map/transpose(jvp(bhqk,bkhd->bqhd))/dot_general | solution.py:48
  252.8 10.0 %fusion.44 = bf16[4,512,1,4,16]{1,4,3,0,2:T(8,128)(2,1)S(1)} fusion(bf16[4,512,1,4,16]{1,0,4,3,2:T(4,128)(2,1)S(1)} %copy-done.15, f32[4,4,512,512]{2,3,1,0:T(8,128)} %get-tuple-element.80, bf16[4,4,512,512]{2,3,1,0:T(8,128)(2,1)} %get-tuple-element.98, f32[4,4,512]{2,1,0:T(4,128)S(1)} %neg.47, f32[4,4,512]{2,1,0:T(4,128)S(1)} %get-tuple-element.79), kind=kOutput, calls=%fused_computation.91 | convolution fusion | flops 155320320 | bytes 25755648 | tf_op jit(solution)/shard_map/transpose(jvp(bqhd,bkhd->bhqk))/dot_general | solution.py:44
  264.5 5.8 fusion.45
  274.9 12.4 %gather_fusion.2 = bf16[4096,64]{1,0:T(8,128)(2,1)S(1)} fusion(bf16[2049,64]{1,0:T(8,128)(2,1)S(1)} %concatenate.7.clone, s32[4096]{0:T(1024)S(1)} %copy-done.26), kind=kCustom, calls=%fused_computation.2 | custom fusion | bytes 1064960 | tf_op jit(solution)/shard_map/gather | solution.py:145
  288.8 5.7 all-to-all-start.5
  295.3 217.7 %all-reduce.13.cloned.1.call-done = (f32[64,192]{1,0:T(8,128)}, f32[64,64]{1,0:T(8,128)}, f32[64,128]{1,0:T(8,128)}) async-done(((f32[64,192]{1,0:T(8,128)}, f32[64,64]{1,0:T(8,128)}, f32[64,128]{1,0:T(8,128)}), (f32[64,192]{1,0:T(8,128)}, f32[64,64]{1,0:T(8,128)}, f32[64,128]{1,0:T(8,128)})) %all-reduce.13.cloned.1.call-update) | async-done | bytes 98320 | tf_op jit(solution)/shard_map/psum | solution.py:224
  517.3 257.3 %all-reduce.15.cloned.1.call-done = (f32[64,256]{1,0:T(8,128)}, f32[256,64]{0,1:T(8,128)}, f32[128,384]{1,0:T(8,128)}, f32[128,128]{1,0:T(8,128)}, f32[128,512]{1,0:T(8,128)}, /*index=5*/f32[512,128]{1,0:T(8,128)}) async-done(((f32[64,256]{1,0:T(8,128)}, f32[256,64]{0,1:T(8,128)}, f32[128,384]{1,0:T(8,128)}, f32[128,128]{1,0:T(8,128)}, f32[128,512]{1,0:T(8,128)}, /*index=5*/f32[512,128]{1,0:T(8,128)}), ...) | async-done | bytes 917520 | tf_op jit(solution)/shard_map/psum | solution.py:224
  784.7 6.2 gather_fusion.3
  (243 shorter events, 70.6 us)
Async XLA Ops:
  7.2 183.8 %copy-start = (bf16[128,512]{1,0:T(8,128)(2,1)S(1)}, bf16[128,512]{1,0:T(8,128)(2,1)}, u32[]{:S(2)}) copy-start(bf16[128,512]{1,0:T(8,128)(2,1)} %param.26) | copy-start | bytes 393220
  10.9 55.4 %copy-start.42 = (s32[512,1]{0,1:T(1,128)}, s32[512,1]{0,1:T(1,128)S(1)}, u32[]{:S(2)}) copy-start(s32[512,1]{0,1:T(1,128)S(1)} %compare_select_fusion.6) | copy-start | bytes 6148
  14.1 41.9 %all-to-all-start = ((s32[64,1,16]{2,1,0:T(1,128)}), s32[64,1,16]{2,1,0:T(1,128)S(1)}, u32[]{:S(2)}, u32[]{:S(2)}) async-start(s32[64,1,16]{2,1,0:T(1,128)} %bitcast.6), calls=%async_computation | async-start | bytes 65536 | tf_op jit(solution)/shard_map/all_to_all | solution.py:201
  26.6 19.3 %copy-start.22 = (s32[1,2048]{1,0:T(1,128)S(1)}, s32[1,2048]{1,0:T(1,128)}, u32[]{:S(2)}) copy-start(s32[1,2048]{1,0:T(1,128)} %param.15) | copy-start | bytes 24580
  26.6 20.1 %copy-start.45 = (s32[1,2048]{1,0:T(1,128)S(1)}, s32[1,2048]{1,0:T(1,128)}, u32[]{:S(2)}) copy-start(s32[1,2048]{1,0:T(1,128)} %param.16) | copy-start | bytes 24580
  26.6 40.3 %copy-start.11 = (bf16[1,2048,64]{1,2,0:T(8,128)(2,1)S(1)}, bf16[1,2048,64]{1,2,0:T(8,128)(2,1)}, u32[]{:S(2)}) copy-start(bf16[1,2048,64]{1,2,0:T(8,128)(2,1)} %param.14) | copy-start | bytes 786436
  47.2 96.9 %copy-start.47 = (f32[512]{0:T(512)}, f32[512]{0:T(512)S(1)}, u32[]{:S(2)}) copy-start(f32[512]{0:T(512)S(1)} %convert_reduce_fusion) | copy-start | bytes 6148
  56.0 20.1 %all-to-all-start.1 = ((s32[64,1,64]{2,1,0:T(1,128)}), s32[64,1,64]{2,1,0:T(1,128)S(1)}, u32[]{:S(2)}, u32[]{:S(2)}) async-start(s32[64,1,64]{2,1,0:T(1,128)} %all_to_all.26), calls=%async_computation.1 | async-start | bytes 65536 | tf_op jit(solution)/shard_map/all_to_all | solution.py:185
  76.1 27.1 %all-to-all-start.2 = ((bf16[64,2,2048]{2,1,0:T(2,128)(2,1)}), bf16[64,2,2048]{2,1,0:T(2,128)(2,1)S(1)}, u32[]{:S(2)}, u32[]{:S(2)}) async-start(bf16[64,2,2048]{2,1,0:T(2,128)(2,1)} %reshape.709), calls=%async_computation.2 | async-start | bytes 1048576 | tf_op jit(solution)/shard_map/all_to_all | solution.py:178
  87.3 29.4 %copy-start.19 = (bf16[64,192]{1,0:T(8,128)(2,1)S(1)}, bf16[64,192]{1,0:T(8,128)(2,1)}, u32[]{:S(2)}) copy-start(bf16[64,192]{1,0:T(8,128)(2,1)} %param.19) | copy-start | bytes 73732
  144.1 35.1 %copy-start.6 = (bf16[2048,256]{1,0:T(8,128)(2,1)}, bf16[2048,256]{1,0:T(8,128)(2,1)S(1)}, u32[]{:S(2)}) copy-start(bf16[2048,256]{1,0:T(8,128)(2,1)S(1)} %get-tuple-element.70) | copy-start | bytes 3145732
  144.1 35.4 %copy-start.10 = (bf16[128,384]{1,0:T(8,128)(2,1)S(1)}, bf16[128,384]{1,0:T(8,128)(2,1)}, u32[]{:S(2)}) copy-start(bf16[128,384]{1,0:T(8,128)(2,1)} %param.24) | copy-start | bytes 294916
  148.1 27.8 %all-to-all-start.3 = ((bf16[64,16,128]{2,1,0:T(8,128)(2,1)}), bf16[64,16,128]{2,1,0:T(8,128)(2,1)S(1)}, u32[]{:S(2)}, u32[]{:S(2)}) async-start(bf16[64,16,128]{2,1,0:T(8,128)(2,1)} %bitcast.25), calls=%async_computation.3 | async-start | bytes 524288 | tf_op jit(solution)/shard_map/all_to_all | solution.py:194
  180.0 9.6 %copy-start.4 = (bf16[512,384]{0,1:T(8,128)(2,1)}, bf16[512,384]{0,1:T(8,128)(2,1)S(1)}, u32[]{:S(2)}) copy-start(bf16[512,384]{0,1:T(8,128)(2,1)S(1)} %convolution_convert_fusion.8) | copy-start | bytes 1179652
  185.0 13.7 %copy-start.27 = (f32[8,512]{1,0:T(8,128)}, f32[8,512]{1,0:T(8,128)S(1)}, u32[]{:S(2)}) copy-start(f32[8,512]{1,0:T(8,128)S(1)} %get-tuple-element.84) | copy-start | bytes 49156
  205.8 13.5 %copy-start.29 = (f32[512]{0:T(512)S(1)}, f32[512]{0:T(512)}, u32[]{:S(2)}) copy-start(f32[512]{0:T(512)} %copy-done.28) | copy-start | bytes 6148
  205.8 13.5 %copy-start.36 = (f32[512]{0:T(512)S(1)}, f32[512]{0:T(512)}, u32[]{:S(2)}) copy-start(f32[512]{0:T(512)} %copy-done.35) | copy-start | bytes 6148
  210.5 18.0 %copy-start.41 = (s32[1024]{0:T(1024)S(1)}, s32[1024]{0:T(1024)}, u32[]{:S(2)}) copy-start(s32[1024]{0:T(1024)} %pad_clamp_fusion) | copy-start | bytes 12292
  210.5 18.0 %all-to-all-start.4 = ((bf16[64,16,128]{2,1,0:T(8,128)(2,1)}), bf16[64,16,128]{2,1,0:T(8,128)(2,1)S(1)}, u32[]{:S(2)}, u32[]{:S(2)}) async-start(bf16[64,16,128]{2,1,0:T(8,128)(2,1)} %bitcast.51), calls=%async_computation.4 | async-start | bytes 524288 | tf_op jit(solution)/shard_map/all_to_all | solution.py:206
  216.4 296.7 %all-reduce.13.cloned.1.call-start = ((), (), s32[]{:S(2)}) async-start(), calls=%async_computation.6 | async-start | bytes 262144 | tf_op jit(solution)/shard_map/psum | solution.py:224
  216.4 13.4 %copy-start.40 = (bf16[64,128]{1,0:T(8,128)(2,1)S(1)}, bf16[64,128]{1,0:T(8,128)(2,1)}, u32[]{:S(2)}) copy-start(bf16[64,128]{1,0:T(8,128)(2,1)} %param.23) | copy-start | bytes 49156
  216.4 13.4 %copy-start.46 = (s32[1,2048]{1,0:T(1,128)S(1)}, s32[1,2048]{1,0:T(1,128)}, u32[]{:S(2)}) copy-start(s32[1,2048]{1,0:T(1,128)} %param.16) | copy-start | bytes 24580
  216.4 13.4 %copy-start.48 = (f32[512]{0:T(512)S(1)}, f32[512]{0:T(512)}, u32[]{:S(2)}) copy-start(f32[512]{0:T(512)} %copy-done.47) | copy-start | bytes 6148
  219.4 12.2 %copy-start.44 = (bf16[256,64]{0,1:T(8,128)(2,1)S(1)}, bf16[256,64]{0,1:T(8,128)(2,1)}, u32[]{:S(2)}) copy-start(bf16[256,64]{0,1:T(8,128)(2,1)} %param.22) | copy-start | bytes 98308
  243.3 19.5 %slice-start = ((s8[16777216]{0:T(1024)(128)(4,1)}), s8[4194304]{0:T(1024)(128)(4,1)S(1)}, s32[]{:S(2)}) async-start(s8[16777216]{0:T(1024)(128)(4,1)} %bitcast.258), calls=%async_computation.8 | async-start | bytes 8388608
  252.7 10.1 %slice-start.1 = ((s8[16777216]{0:T(1024)(128)(4,1)}), s8[4194304]{0:T(1024)(128)(4,1)S(1)}, s32[]{:S(2)}) async-start(s8[16777216]{0:T(1024)(128)(4,1)} %bitcast.258), calls=%async_computation.9 | async-start | bytes 8388608
  252.7 10.6 %slice-start.2 = ((s8[16777216]{0:T(1024)(128)(4,1)}), s8[4194304]{0:T(1024)(128)(4,1)S(1)}, s32[]{:S(2)}) async-start(s8[16777216]{0:T(1024)(128)(4,1)} %bitcast.258), calls=%async_computation.10 | async-start | bytes 8388608
  252.7 11.8 %slice-start.3 = ((s8[16777216]{0:T(1024)(128)(4,1)}), s8[4194304]{0:T(1024)(128)(4,1)S(1)}, s32[]{:S(2)}) async-start(s8[16777216]{0:T(1024)(128)(4,1)} %bitcast.258), calls=%async_computation.11 | async-start | bytes 8388608
  252.7 11.8 %copy-start.13 = (bf16[4,512,1,4,16]{1,0,4,3,2:T(4,128)(2,1)S(1)}, bf16[4,512,1,4,16]{1,0,4,3,2:T(4,128)(2,1)}, u32[]{:S(2)}) copy-start(bf16[4,512,1,4,16]{1,0,4,3,2:T(4,128)(2,1)} %copy-done.12) | copy-start | bytes 786436
  288.8 495.1 %all-to-all-start.5 = ((bf16[64,2,2048]{2,1,0:T(2,128)(2,1)}), bf16[64,2,2048]{2,1,0:T(2,128)(2,1)S(1)}, u32[]{:S(2)}, u32[]{:S(2)}) async-start(bf16[64,2,2048]{2,1,0:T(2,128)(2,1)} %reshape.711), calls=%async_computation.5 | async-start | bytes 1048576 | tf_op jit(solution)/shard_map/all_to_all | solution.py:216
  294.6 490.1 %copy-start.34 = (s32[2048]{0:T(1024)S(1)}, s32[2048]{0:T(1024)}, u32[]{:S(2)}) copy-start(s32[2048]{0:T(1024)} %broadcast_clamp_fusion.1) | copy-start | bytes 24580
  294.6 480.0 %all-reduce.15.cloned.1.call-start = ((), (), s32[]{:S(2)}) async-start(), calls=%async_computation.7 | async-start | bytes 1835008 | tf_op jit(solution)/shard_map/psum | solution.py:224
  (31 other events, 106.1 us)
Sparse Core Ops, SparseCore 0:
  273.2 239.8 all-reduce.12
  520.1 254.4 all-reduce.14
where the time goes:
time: 812 us; the launch traced here: 799 us
  waiting for transfers between devices  510 us (63%)
  matrix products  82.4 us (10%)
  local copies, waits for them, and re-layouts  75.2 us (9%)
  starting transfers between devices  59.8 us (7%)
  other arithmetic  55.5 us (7%)
  between operations  15.7 us (2%)
    psum x2, waiting for transfers between devices, shards(): lax.psum((grads_first[0], grads_first[1], grads_first[2], grads_first[3],...  475 us
    dot_general x4, matrix products, block(): jnp.einsum('bqhd,bkhd->bhqk', parted[:, :, 0], parted[:, :, 1], preferred...  20.4 us
    another operation x4, other arithmetic  19.6 us
    dot_general x6, matrix products, block(): jnp.einsum('bhqk,bkhd->bqhd', softmax_weights, parted[:, :, 2], preferred...  19.4 us
    gather x2, local copies, waits for them, and re-layouts, take_rows(): return padded[landing.reshape(-1)].reshape(devices, capacity, feature_width)  17 us
  transfers between devices with their start and end apart: 8, of which 5 were waited for; matrix products, arithmetic and copies ran while one was open for 9% of the time, Pallas kernels for 0%

commit v1 on v0

v1 whole, which is shorter than its diff:
```python
import math

import jax
import jax.numpy as jnp
from jax import lax
from jax.experimental import pallas as pl
from jax.experimental.pallas import tpu as pltpu
from jax.sharding import PartitionSpec as P


HEAD = 16
PATCH = 512
PATCHES = 4
ROWS = 2048
COARSE = 512
PEERS = 64
NEAR, FAR = 8, 32
MESH = pl.DeviceIdType.MESH
SHARPEN = HEAD**-0.5 / math.log(2.0)
f32, bf16, i32 = jnp.float32, jnp.bfloat16, jnp.int32


def dot(left, right):
    return jnp.dot(left, right, preferred_element_type=f32)


def dot_nt(left, right):
    return lax.dot_general(left, right, (((1,), (1,)), ((), ())), preferred_element_type=f32)


def turned(array):
    return array.astype(f32).T.astype(bf16)


def rows_of(count, width):
    return lax.broadcasted_iota(i32, (count, width), 0)


def match(row, count):
    return jnp.where(rows_of(count, row.shape[1]) == row, 1.0, 0.0).astype(bf16)


def norm(values):
    centred = values - jnp.mean(values, axis=0, keepdims=True)
    rate = lax.rsqrt(jnp.mean(centred * centred, axis=0, keepdims=True) + 1e-05)
    return centred * rate, rate


def norm_back(gradient, normed, rate):
    mean = jnp.mean(gradient, axis=0, keepdims=True)
    along = jnp.mean(gradient * normed, axis=0, keepdims=True)
    return rate * (gradient - mean - normed * along)


def gelu_parts(values):
    below = 0.5 + 0.5 * lax.erf(values * math.sqrt(0.5))
    bell = jnp.exp(-0.5 * values * values) * (1.0 / math.sqrt(2.0 * math.pi))
    return values * below, below + values * bell


def only(array, head):
    width = array.shape[1]
    parts = []
    if head > 0:
        parts.append(jnp.zeros((HEAD * head, width), array.dtype))
    parts.append(array[HEAD * head : HEAD * (head + 1)])
    rest = array.shape[0] - HEAD * (head + 1)
    if rest > 0:
        parts.append(jnp.zeros((rest, width), array.dtype))
    return jnp.concatenate(parts, axis=0)


def attend(mixed, width):
    keys = turned(mixed[width : 2 * width])
    ones = jnp.ones((HEAD, PATCH), bf16)
    outs, logs = [], []
    for head in range(width // HEAD):
        scores = dot(keys, only(mixed[:width], head))
        top = jnp.max(scores, axis=0, keepdims=True)
        powers = jnp.exp2((scores - top) * SHARPEN).astype(bf16)
        start = 2 * width + HEAD * head
        sums = dot(jnp.concatenate([mixed[start : start + HEAD], ones], axis=0), powers)
        size = sums[HEAD : HEAD + 1]
        outs.append(sums[:HEAD] / size)
        logs.append(top * SHARPEN + jnp.log2(size))
    return jnp.concatenate(outs, axis=0).astype(bf16), logs


def attend_back(mixed, attended, gradient, logs, width):
    keys = turned(mixed[width : 2 * width])
    values = turned(mixed[2 * width :])
    grad_queries, grad_keys, grad_values = [], [], []
    for head in range(width // HEAD):
        part = slice(HEAD * head, HEAD * (head + 1))
        queries = mixed[part]
        key_rows = mixed[width + HEAD * head : width + HEAD * (head + 1)]
        grad = gradient[part]
        overlap = jnp.sum(
            grad.astype(f32) * attended[part].astype(f32), axis=0, keepdims=True
        )
        scores = dot(keys, only(mixed[:width], head))
        probs = jnp.exp2(scores * SHARPEN - logs[head])
        spread = dot(values, only(gradient, head))
        change = (probs * (spread - overlap)).astype(bf16)
        grad_queries.append(dot(key_rows, change) * HEAD**-0.5)
        grad_keys.append(dot_nt(queries, change) * HEAD**-0.5)
        grad_values.append(dot_nt(grad, probs.astype(bf16)))
    return jnp.concatenate(grad_queries + grad_keys + grad_values, axis=0).astype(bf16)


def block_front(inputs, inlet_t, outlet_t, widen_t, narrow_t):
    width = inputs.shape[0]
    start = inputs.astype(f32)
    normed = norm(start)[0].astype(bf16)
    mixed = dot(inlet_t, normed).astype(bf16)
    attended, logs = attend(mixed, width)
    middle = start + dot(outlet_t, attended)
    second = norm(middle)[0].astype(bf16)
    hidden, slope = gelu_parts(dot(widen_t, second))
    hidden = hidden.astype(bf16)
    result = (middle + dot(narrow_t, hidden)).astype(bf16)
    return result, mixed, attended, logs, hidden, slope.astype(bf16)


def block_back(inputs, mixed, attended, logs, hidden, slope, gradient, weights, outlet_t):
    inlet, outlet, widen, narrow = weights
    width = inputs.shape[0]
    start = inputs.astype(f32)
    normed, rate = norm(start)
    second, rate_two = norm(start + dot(outlet_t, attended))
    grad_narrow = dot_nt(gradient, hidden)
    grad_wide = (dot(narrow, gradient) * slope.astype(f32)).astype(bf16)
    grad_widen = dot_nt(second.astype(bf16), grad_wide)
    grad_middle = gradient.astype(f32) + norm_back(dot(widen, grad_wide), second, rate_two)
    short = grad_middle.astype(bf16)
    grad_outlet = dot_nt(attended, short)
    grad_attended = dot(outlet, short).astype(bf16)
    grad_mixed = attend_back(mixed, attended, grad_attended, logs, width)
    grad_inlet = dot_nt(normed.astype(bf16), grad_mixed)
    grad_inputs = grad_middle + norm_back(dot(inlet, grad_mixed), normed, rate)
    return grad_inputs.astype(bf16), grad_inlet, grad_outlet, grad_widen, grad_narrow


def ranks(owner):
    before_me = jnp.where(rows_of(256, 256) < lax.broadcasted_iota(i32, (256, 256), 1), 1.0, 0.0)
    before_me = before_me.astype(bf16)
    before = jnp.zeros((PEERS, 1), f32)
    found = []
    for start in range(0, owner.shape[1], 256):
        hits = jnp.where(rows_of(PEERS, 256) == owner[:, start : start + 256], 1.0, 0.0)
        count = dot(hits.astype(bf16), before_me) + before
        found.append(jnp.sum(hits * count, axis=0, keepdims=True))
        before = before + jnp.sum(hits, axis=1, keepdims=True)
    return jnp.concatenate(found, axis=1).astype(i32)


def marks(owner, rank, value):
    hits = match(owner, PEERS)
    at = rows_of(128, owner.shape[1]) == rank
    high = jnp.where(at, (value >> 6).astype(f32), 0.0).astype(bf16)
    low = jnp.where(at, (value & 63).astype(f32), 0.0).astype(bf16)
    return dot_nt(hits, high) * 64.0 + dot_nt(hits, low)


def spread_places(table):
    lane = lax.broadcasted_iota(i32, (PEERS, 128), 1)
    apart = table + jnp.where(lane >= 64, 4096.0, 0.0)
    over = jnp.zeros((PEERS, 128), f32)
    for shift in range(1, 64):
        over = jnp.where(apart == pltpu.roll(apart, 128 - shift, 1), 1.0, over)
    high = jnp.floor(table * (1.0 / 64.0))
    low = table - 64.0 * high
    high = high + 64.0 * over
    stack = []
    for part in range(5):
        stack += [high[:, 16 * part : 16 * part + 16], low[:, 16 * part : 16 * part + 16]]
    stack = jnp.concatenate(stack, axis=0).astype(bf16)
    column = lax.broadcasted_iota(i32, (16, 1024), 1)
    spread = dot(stack, jnp.where(column % 16 == rows_of(16, 1024), 1.0, 0.0).astype(bf16))
    own = rows_of(PEERS, 1024) == lax.broadcasted_iota(i32, (PEERS, 1024), 1) // 16
    places, drops = [], []
    for part in range(5):
        high = jnp.sum(jnp.where(own, spread[128 * part : 128 * part + 64], 0.0), axis=0, keepdims=True)
        low = jnp.sum(jnp.where(own, spread[128 * part + 64 : 128 * part + 128], 0.0), axis=0, keepdims=True)
        drops.append(high > 63.5)
        high = jnp.where(high > 63.5, high - 64.0, high)
        places.append((high * 64.0 + low).astype(i32) - 1)
    return places, drops


def last_senders(inside, hits):
    width = hits[0].shape[0]
    count = len(inside[0])
    sender = lax.broadcasted_iota(i32, (1, 1024), 1) // 16
    own = rows_of(PEERS, 1024) == sender
    seen = jnp.zeros((PEERS * count, width), f32)
    for masks, hit in zip(inside, hits):
        wide = [jnp.where(own & mask, 1.0, 0.0) for mask in masks]
        seen += dot_nt(jnp.concatenate(wide, axis=0).astype(bf16), hit)
    index = rows_of(PEERS, width).astype(f32)
    lasts = []
    for part in range(count):
        lasts.append(jnp.max(jnp.where(seen[PEERS * part : PEERS * part + PEERS] > 0.5, index, -1.0), axis=0, keepdims=True))
    lasts = jnp.concatenate(lasts + [jnp.zeros((16 - count, width), f32)], axis=0).astype(bf16)
    found = []
    for masks, hit in zip(inside, hits):
        got = dot(lasts, hit)
        mine = jnp.full((1, 1024), -1.0, f32)
        for part in range(count):
            mine = jnp.where(masks[part], got[part : part + 1], mine)
        found.append(mine == sender.astype(f32))
    return found


def greet_peers(me):
    barrier = pltpu.get_barrier_semaphore()

    def greet(step, carry):
        pl.semaphore_signal(
            barrier, device_id={"pts": (me + step) % PEERS}, device_id_type=MESH
        )
        return carry

    lax.fori_loop(1, PEERS, greet, 0)
    return barrier


def exchange(me, source, target, send_sem, recv_sem):

    def send(step, carry):
        other = (me + step) % PEERS
        pltpu.make_async_remote_copy(
            source.at[other],
            target.at[me],
            send_sem,
            recv_sem,
            device_id={"pts": other},
            device_id_type=MESH,
        ).start()
        return carry

    lax.fori_loop(1, PEERS, send, 0)
    target[me] = source[me]
    return pltpu.make_async_remote_copy(
        source.at[pl.ds(0, PEERS - 1)],
        target.at[pl.ds(0, PEERS - 1)],
        send_sem,
        recv_sem,
        device_id={"pts": me},
        device_id_type=MESH,
    )


def pack_kernel(feats_ref, first_ref, second_ref, rows_ref, places_ref, slot_one_ref, slot_two_ref, send, mark, sems):
    me = lax.axis_index("pts")
    barrier = greet_peers(me)
    first, second = first_ref[...], second_ref[...]
    owner_one, owner_two = first // ROWS, second // COARSE
    rank_one, rank_two = ranks(owner_one), ranks(owner_two)
    found = marks(owner_one, rank_one, first % ROWS + 1)
    found += marks(owner_two, rank_two + 64, second % COARSE + 1)
    mark[:, 0, :] = found
    pl.semaphore_wait(barrier, PEERS - 1)
    marked = exchange(me, mark, places_ref, sems.at[0], sems.at[1])
    slot = owner_one * 16 + rank_one % 16
    layer = rank_one // 16
    slot_one_ref[...] = jnp.concatenate([slot, layer], axis=0)
    slot_two_ref[...] = owner_two * 16 + rank_two
    feats = feats_ref[...].astype(f32).T
    wide = [jnp.where(layer == index, feats, 0.0) for index in range(4)]
    wide = jnp.concatenate(wide, axis=0).astype(bf16)
    send[...] = dot_nt(match(slot, 1024), wide).astype(bf16).reshape(PEERS, 16, 256)
    moved = exchange(me, send, rows_ref, sems.at[2], sems.at[3])
    marked.wait_recv()
    moved.wait_recv()
    marked.wait_send()
    moved.wait_send()


def front_kernel(
    rows_ref, places_ref, ident_ref, slot_ref, inlet_ref, outlet_ref, widen_ref, narrow_ref, pool_ref,
    send_ref, places_out, inputs_ref, mixed_ref, attended_ref, logs_ref, hidden_ref, slope_ref, pooled_ref, sizes_ref,
    total_ref,
):
    places, drops = spread_places(places_ref[...])
    for part in range(5):
        places_out[part : part + 1, :] = places[part]
    kept = [jnp.where(drop, -1, place) for place, drop in zip(places, drops)]
    hits = [match(place % 512, 512) for place in kept[:4]]
    last = last_senders([[place // 512 == patch for patch in range(PATCHES)] for place in kept[:4]], hits)
    kept_two = match(kept[4], COARSE)
    last_two = last_senders([[kept[4] >= 0]], [kept_two])
    places_out[5:6, :] = jnp.where(last_two[0], kept[4], -1)

    arrived = rows_ref[...].astype(f32).T
    landed = jnp.zeros((256, 512), f32)
    for layer in range(4):
        place = jnp.where(last[layer], kept[layer], -1)
        feats = arrived[64 * layer : 64 * layer + 64]
        wide = [jnp.where(place // 512 == patch, feats, 0.0) for patch in range(PATCHES)]
        wide = jnp.concatenate(wide, axis=0).astype(bf16)
        landed += dot_nt(wide, hits[layer])
    inputs_ref[...] = landed.astype(bf16).reshape(PATCHES, 64, PATCH)

    turned_weights = [turned(ref[...]) for ref in (inlet_ref, outlet_ref, widen_ref, narrow_ref)]
    total_ref[...] = jnp.zeros_like(total_ref)

    def step(patch, carry):
        result, mixed, attended, logs, hidden, slope = block_front(inputs_ref[patch], *turned_weights)
        mixed_ref[patch] = mixed
        attended_ref[patch] = attended
        logs_ref[patch] = jnp.concatenate(logs, axis=0)
        hidden_ref[patch] = hidden
        slope_ref[patch] = slope
        ident = ident_ref[:, pl.ds(pl.multiple_of(patch * PATCH, PATCH), PATCH)]
        counted = jnp.concatenate([result, jnp.ones((16, PATCH), bf16)], axis=0)
        total_ref[...] += dot_nt(counted, match(ident, COARSE))
        return carry

    lax.fori_loop(0, PATCHES, step, 0)
    sizes = total_ref[64:65]
    pooled = (total_ref[:64] / sizes).astype(bf16)
    pooled_ref[...] = pooled
    sizes_ref[...] = sizes
    coarse = dot(turned(pool_ref[...]), pooled).astype(bf16)
    send_ref[...] = dot_nt(match(slot_ref[...], 1024), coarse).astype(bf16)


def exchange_kernel(source_ref, target_ref, sems):
    me = lax.axis_index("pts")
    barrier = greet_peers(me)
    pl.semaphore_wait(barrier, PEERS - 1)
    moved = exchange(me, source_ref, target_ref, sems.at[0], sems.at[1])
    moved.wait_recv()
    moved.wait_send()


def store_lanes(ref, row, array):
    height = array.shape[0]
    for index in range(array.shape[1] // 128):
        start = row + height * index
        ref[start : start + height, :] = array[:, 128 * index : 128 * index + 128].astype(ref.dtype)


def middle_kernel(
    rows_ref, places_ref, cotangent_ref, inlet_ref, outlet_ref, widen_ref, narrow_ref,
    second_ref, send_ref, grads_ref,
):
    inputs = dot_nt(turned(rows_ref[...]), match(places_ref[5:6, :], COARSE)).astype(bf16)
    weights = [ref[...] for ref in (inlet_ref, outlet_ref, widen_ref, narrow_ref)]
    turned_weights = [turned(weight) for weight in weights]
    result, mixed, attended, logs, hidden, slope = block_front(inputs, *turned_weights)
    second_ref[...] = turned(result)
    gradient = turned(cotangent_ref[...])
    back, grad_inlet, grad_outlet, grad_widen, grad_narrow = block_back(
        inputs, mixed, attended, logs, hidden, slope, gradient, weights, turned_weights[1]
    )
    send_ref[...] = turned(dot(back, match(places_ref[4:5, :], COARSE)))
    store_lanes(grads_ref, 0, grad_inlet)
    store_lanes(grads_ref, 384, grad_outlet)
    store_lanes(grads_ref, 512, grad_widen)
    store_lanes(grads_ref, 1024, grad_narrow)


def back_kernel(
    rows_ref, slot_ref, places_ref, ident_ref, inputs_ref, mixed_ref, attended_ref, logs_ref, hidden_ref, slope_ref,
    pooled_ref, sizes_ref, inlet_ref, outlet_ref, widen_ref, narrow_ref, pool_ref,
    send_ref, grads_ref,
    back_ref, front_total, widen_total, narrow_total,
):
    grad_coarse = dot(turned(rows_ref[...]), match(slot_ref[...], 1024)).astype(bf16)
    grad_pool = dot_nt(pooled_ref[...], grad_coarse)
    grad_pooled = dot(pool_ref[...], grad_coarse).astype(bf16).astype(f32)
    share = (grad_pooled / sizes_ref[...]).astype(bf16)
    weights = [ref[...] for ref in (inlet_ref, outlet_ref, widen_ref, narrow_ref)]
    outlet_t = turned(weights[1])
    front_total[...] = jnp.zeros_like(front_total)
    widen_total[...] = jnp.zeros_like(widen_total)
    narrow_total[...] = jnp.zeros_like(narrow_total)

    def step(patch, carry):
        ident = ident_ref[:, pl.ds(pl.multiple_of(patch * PATCH, PATCH), PATCH)]
        gradient = dot(share, match(ident, COARSE)).astype(bf16)
        logs = [logs_ref[patch, head : head + 1, :] for head in range(4)]
        back, grad_inlet, grad_outlet, grad_widen, grad_narrow = block_back(
            inputs_ref[patch], mixed_ref[patch], attended_ref[patch], logs, hidden_ref[patch], slope_ref[patch],
            gradient, weights, outlet_t,
        )
        back_ref[patch] = back
        front_total[...] += jnp.concatenate([grad_inlet, grad_outlet], axis=1)
        widen_total[...] += grad_widen
        narrow_total[...] += grad_narrow
        return carry

    lax.fori_loop(0, PATCHES, step, 0)
    store_lanes(grads_ref, 0, front_total[...])
    store_lanes(grads_ref, 128, widen_total[...])
    store_lanes(grads_ref, 256, narrow_total[...])
    store_lanes(grads_ref, 384, grad_pool)
    grads_ref[448:, :] = jnp.zeros((64, 128), grads_ref.dtype)
    back = back_ref[...].reshape(256, PATCH)
    taken = []
    for layer in range(4):
        place = places_ref[layer : layer + 1, :]
        found = dot(back, match(place % 512, 512))
        parts = [jnp.where(place // 512 == patch, found[64 * patch : 64 * patch + 64], 0.0) for patch in range(PATCHES)]
        taken.append(parts[0] + parts[1] + parts[2] + parts[3])
    send_ref[...] = jnp.concatenate(taken, axis=0).T.astype(bf16)


def final_kernel(
    scale, source_ref, early_ref, late_ref, target_ref, out_ref,
    half, near, middle, far, chunk, whole, near_out, sems,
):
    me, rep = lax.axis_index("pts"), lax.axis_index("rep")
    place, core = me // 2, me % 2
    mine = core * 4 + rep

    def near_device(step):
        other = (mine + step) % NEAR
        return other, {"pts": place * 2 + other // 4, "rep": other % 4}

    def far_device(step):
        other = (place + step) % FAR
        return other, {"pts": other * 2 + core}

    def copy_to(source, target, index, device):
        return pltpu.make_async_remote_copy(
            source, target, sems.at[index], sems.at[index + 1], device_id=device, device_id_type=MESH
        )

    def batch_of(target, count, index):
        some = target.at[pl.ds(0, count - 1)]
        return copy_to(some, some, index, {"pts": me})

    barrier = greet_peers(me)

    def greet_near(step, carry):
        pl.semaphore_signal(barrier, device_id=near_device(step)[1], device_id_type=MESH)
        return carry

    lax.fori_loop(1, NEAR, greet_near, 0)
    half[:6] = early_ref[...]
    half[6:] = late_ref[...]
    pl.semaphore_wait(barrier, PEERS + NEAR - 2)

    def send_near(step, carry):
        other, device = near_device(step)
        copy_to(half.at[other], near.at[mine], 0, device).start()
        return carry

    lax.fori_loop(1, NEAR, send_near, 0)
    moved = exchange(me, source_ref, target_ref, sems.at[8], sems.at[9])
    near[mine] = half[mine]
    batch_near = batch_of(near, NEAR, 0)
    batch_near.wait_recv()
    total = near[0].astype(f32)
    for index in range(1, NEAR):
        total = total + near[index].astype(f32)
    middle[...] = total.reshape(FAR, 8, 128)

    def send_far(step, carry):
        other, device = far_device(step)
        copy_to(middle.at[other], far.at[place], 2, device).start()
        return carry

    lax.fori_loop(1, FAR, send_far, 0)
    far[place] = middle[place]
    batch_far = batch_of(far, FAR, 2)
    batch_far.wait_recv()
    chunk[...] = jnp.sum(far[...], axis=0) * scale

    def spread_far(step, carry):
        copy_to(chunk, whole.at[place], 4, far_device(step)[1]).start()
        return carry

    lax.fori_loop(1, FAR, spread_far, 0)
    whole[place] = chunk[...]
    batch_whole = batch_of(whole, FAR, 4)
    batch_whole.wait_recv()
    near_out[...] = whole[...].reshape(256, 128).astype(bf16)

    def spread_near(step, carry):
        copy_to(near_out, out_ref.at[mine], 6, near_device(step)[1]).start()
        return carry

    lax.fori_loop(1, NEAR, spread_near, 0)
    out_ref[mine] = near_out[...]
    batch_out = batch_of(out_ref, NEAR, 6)
    batch_out.wait_recv()
    moved.wait_recv()
    moved.wait_send()
    batch_near.wait_send()
    batch_far.wait_send()
    batch_whole.wait_send()
    batch_out.wait_send()


def load_lanes(ref, row, height, count):
    parts = [ref[row + height * index : row + height * (index + 1), :].astype(f32) for index in range(count)]
    return jnp.concatenate(parts, axis=1) if count > 1 else parts[0]


def output_kernel(
    rows_ref, slot_ref, grads_ref,
    feats_ref, inlet_one, outlet_one, widen_one, narrow_one, pool, inlet_two, outlet_two, widen_two, narrow_two,
):
    slot, layer = slot_ref[0:1, :], slot_ref[1:2, :]
    found = dot(turned(rows_ref[...]), match(slot, 1024))
    parts = [jnp.where(layer == index, found[64 * index : 64 * index + 64], 0.0) for index in range(4)]
    feats_ref[...] = (parts[0] + parts[1] + parts[2] + parts[3]).T.astype(bf16)
    front = load_lanes(grads_ref, 1536, 64, 2)
    inlet_one[...] = front[:, :192]
    outlet_one[...] = front[:, 192:]
    widen_one[...] = load_lanes(grads_ref, 1664, 64, 2)
    narrow_one[...] = load_lanes(grads_ref, 1792, 64, 2).T
    pool[...] = load_lanes(grads_ref, 1920, 64, 1)
    inlet_two[...] = load_lanes(grads_ref, 0, 128, 3)
    outlet_two[...] = load_lanes(grads_ref, 384, 128, 1)
    widen_two[...] = load_lanes(grads_ref, 512, 128, 4)
    narrow_two[...] = load_lanes(grads_ref, 1024, 128, 4).T


def call(kernel, outs, scratch, *operands, collective=None):
    params = {} if collective is None else {"collective_id": collective, "has_side_effects": True}
    whole = pl.BlockSpec(memory_space=pltpu.VMEM)
    return pl.pallas_call(
        kernel,
        out_shape=[jax.ShapeDtypeStruct(shape, dtype) for shape, dtype in outs],
        in_specs=[whole] * len(operands),
        out_specs=[whole] * len(outs),
        scratch_shapes=scratch,
        compiler_params=pltpu.CompilerParams(vmem_limit_bytes=56 * 2**20, **params),
    )(*operands)


def shards(
    feats,
    dest_first,
    pool_ids,
    dest_second,
    cotangent,
    inlet_first,
    outlet_first,
    widen_first,
    narrow_first,
    pool_weight,
    inlet_second,
    outlet_second,
    widen_second,
    narrow_second,
):
    first = (inlet_first, outlet_first, widen_first, narrow_first)
    second = (inlet_second, outlet_second, widen_second, narrow_second)
    rows, places, slot_one, slot_two = call(
        pack_kernel,
        [((PEERS, 16, 256), bf16), ((PEERS, 1, 128), f32), ((2, ROWS), i32), ((1, COARSE), i32)],
        [
            pltpu.VMEM((PEERS, 16, 256), bf16),
            pltpu.VMEM((PEERS, 1, 128), f32),
            pltpu.SemaphoreType.DMA((4,)),
        ],
        feats[0], dest_first, dest_second,
        collective=1,
    )
    send, places, *saved = call(
        front_kernel,
        [
            ((1024, 128), bf16),
            ((6, 1024), i32),
            ((PATCHES, 64, PATCH), bf16),
            ((PATCHES, 192, PATCH), bf16),
            ((PATCHES, 64, PATCH), bf16),
            ((PATCHES, 4, PATCH), f32),
            ((PATCHES, 256, PATCH), bf16),
            ((PATCHES, 256, PATCH), bf16),
            ((64, COARSE), bf16),
            ((1, COARSE), f32),
        ],
        [pltpu.VMEM((80, COARSE), f32)],
        rows.reshape(1024, 256), places.reshape(PEERS, 128), pool_ids, slot_two, *first, pool_weight,
    )

    def move(array, collective):
        return call(
            exchange_kernel,
            [((PEERS, 16, 128), bf16)],
            [pltpu.SemaphoreType.DMA((2,))],
            array.reshape(PEERS, 16, 128),
            collective=collective,
        )[0].reshape(1024, 128)

    second_out, send, grads_second = call(
        middle_kernel,
        [((COARSE, 128), bf16), ((1024, 128), bf16), ((1536, 128), bf16)],
        [],
        move(send, 2), places, cotangent[0], *second,
    )
    send, grads_first = call(
        back_kernel,
        [((1024, 256), bf16), ((512, 128), bf16)],
        [
            pltpu.VMEM((PATCHES, 64, PATCH), bf16),
            pltpu.VMEM((64, 256), f32),
            pltpu.VMEM((64, 256), f32),
            pltpu.VMEM((64, 256), f32),
        ],
        move(send, 3), slot_two, places, pool_ids, *saved, *first, pool_weight,
    )
    scale = 1.0 / math.sqrt(lax.axis_size("rep") * lax.axis_size("pts") * COARSE)
    rows, grads = call(
        lambda *refs: final_kernel(scale, *refs),
        [((PEERS, 16, 256), bf16), ((NEAR, 256, 128), bf16)],
        [
            pltpu.VMEM((NEAR, 256, 128), bf16),
            pltpu.VMEM((NEAR, 256, 128), bf16),
            pltpu.VMEM((FAR, 8, 128), f32),
            pltpu.VMEM((FAR, 8, 128), f32),
            pltpu.VMEM((8, 128), f32),
            pltpu.VMEM((FAR, 8, 128), f32),
            pltpu.VMEM((256, 128), bf16),
            pltpu.SemaphoreType.DMA((10,)),
        ],
        send.reshape(PEERS, 16, 256), grads_second.reshape(6, 256, 128), grads_first.reshape(2, 256, 128),
        collective=4,
    )
    feats_grad, *totals = call(
        output_kernel,
        [((ROWS, 64), bf16)]
        + [
            (weight.shape, f32)
            for weight in first + (pool_weight,) + second
        ],
        [],
        rows.reshape(1024, 256), slot_one, grads.reshape(2048, 128),
    )
    return (second_out[None], feats_grad[None], *totals)


def solution(mesh):
    split = P("rep", "pts")
    return jax.shard_map(
        shards,
        mesh=mesh,
        in_specs=(split,) * 5 + (P(),) * 9,
        out_specs=(split,) * 2 + (P(),) * 9,
        check_vma=False,
    )
```

time: 812 us -> 168 us (0.21); the launches traced: 799 us -> 168 us
  waiting for transfers between devices: 510 us -> 0 us
  Pallas kernels: 0 us -> 161 us
  matrix products: 82.4 us -> 0 us
  local copies, waits for them, and re-layouts: 75.2 us -> 6.13 us
  starting transfers between devices: 59.8 us -> 0 us
  other arithmetic: 55.5 us -> 0 us
  between operations: 15.7 us -> 0.68 us
    psum x2 -> x0, waiting for transfers between devices: 475 us -> none  [shards(): lax.psum((grads_first[0], grads_first[1], grads_first[2], grads_first[3],...]
    pallas_call x0 -> x8, Pallas kernels: none -> 161 us  [call(): pl.pallas_call(kernel, out_shape=[jax.ShapeDtypeStruct(shape, dtype) for...]
    dot_general x37 -> x0, matrix products: 68.7 us -> none  [the longest x4 20.4 us: block(): jnp.einsum('bqhd,bkhd->bhqk', parted[:, :, 0], parted[:, :, 1], preferred...]
    all_to_all x6 -> x0, starting transfers between devices: 59.8 us -> none  [the longest x1 15.8 us: shards(): lax.all_to_all(shortened(fill_slots(coarse_in, slot_two, devices, capacit...]
    all_to_all x6 -> x0, waiting for transfers between devices: 34.7 us -> none  [the longest x1 15.9 us: shards(): lax.all_to_all(fill_slots(point_rows, slot_one, devices, capacity_one), '...]
    scatter x6 -> x0, local copies, waits for them, and re-layouts: 33.5 us -> none  [the longest x2 14.4 us: land_rows(): placed = jnp.zeros((row_count + 1, feature_width), arrived.dtype).at[land...]
    gather x4 -> x0, local copies, waits for them, and re-layouts: 24.5 us -> none  [the longest x2 17 us: take_rows(): return padded[landing.reshape(-1)].reshape(devices, capacity, feature_width)]
    another operation x4 -> x0, other arithmetic: 19.6 us -> none
  transfers between devices with their start and end apart: 8 -> 0, of which waited for: 5 -> 0; matrix products, arithmetic and copies ran while one was open for 9% -> 0% of each run, Pallas kernels for 0% -> 0%
where the time goes in v1:
time: 168 us
  Pallas kernels  161 us (96%)
  local copies, waits for them, and re-layouts  6.13 us (4%)
    pallas_call x8, Pallas kernels, call(): pl.pallas_call(kernel, out_shape=[jax.ShapeDtypeStruct(shape, dtype) for...  161 us
    unnamed x6, local copies, waits for them, and re-layouts  6.13 us

profile of v1, /device:TPU:32, one launch (start us, length us, event | category | flops | bytes accessed | tf_op | source)
XLA Modules:
  0.0 167.7 jit_solution(16925846770041660314)
XLA Ops:
  0.6 1.5 copy.26.narrow_ref
  2.1 2.0 %copy.25 = bf16[1,2048,64]{2,1,0:T(8,128)(2,1)} copy(bf16[1,2048,64]{1,2,0:T(8,128)(2,1)} %param.14) | data formatting | bytes 524288 | tf_op args[0]
  4.1 26.7 %shard_map.221 = (bf16[64,16,256]{2,1,0:T(8,128)(2,1)}, f32[64,1,128]{2,1,0:T(1,128)}, s32[2,2048]{1,0:T(2,128)}, s32[1,512]{1,0:T(1,128)}) custom-call(bf16[2048,64]{1,0:T(8,128)(2,1)} %bitcast.15, s32[1,2048]{1,0:T(1,128)} %first_ref.1, s32[1,512]{1,0:T(1,128)} %second_ref.1), custom_call_target="tpu_custom_call" | custom-call | tf_op jit(solution)/shard_map/pallas_call | solution.py:527
  30.8 19.4 %shard_map.222 = (bf16[1024,128]{1,0:T(8,128)(2,1)}, s32[6,1024]{1,0:T(8,128)}, bf16[4,64,512]{2,1,0:T(8,128)(2,1)}, bf16[4,192,512]{2,1,0:T(8,128)(2,1)}, bf16[...) custom-call(bf16[1024,256]{1,0:T(8,128)(2,1)} %bitcast.22, ...), custom_call_target="tpu_custom_call" | custom-call | tf_op jit(solution)/shard_map/pallas_call | solution.py:527
  50.2 17.1 %shard_map.223 = bf16[64,16,128]{2,1,0:T(8,128)(2,1)} custom-call(bf16[64,16,128]{2,1,0:T(8,128)(2,1)} %bitcast.24), custom_call_target="tpu_custom_call" | custom-call | tf_op jit(solution)/shard_map/pallas_call | solution.py:527
  67.3 13.9 %shard_map.224 = (bf16[512,128]{1,0:T(8,128)(2,1)}, bf16[1024,128]{1,0:T(8,128)(2,1)}, bf16[1536,128]{1,0:T(8,128)(2,1)}) custom-call(bf16[1024,128]{1,0:T(8,128)(2,1)} %bitcast.17, s32[6,1024]{1,0:T(8,128)} %get-tuple-element.46.places_ref, bf16[512,128]{1,0:T(8,128)(2,1)} %bitcast.26, bf16[128,384]{1,0:T(8,128)(2,1)} %inlet_ref.4, ...), custom_call_target="tpu_custom_call" | custom-call | tf_op jit(solution)/shard_map/pallas_call | solution.py:527
  81.3 16.8 %shard_map.225 = bf16[64,16,128]{2,1,0:T(8,128)(2,1)} custom-call(bf16[64,16,128]{2,1,0:T(8,128)(2,1)} %bitcast.25), custom_call_target="tpu_custom_call" | custom-call | tf_op jit(solution)/shard_map/pallas_call | solution.py:527
  98.1 20.2 %shard_map.226 = (bf16[1024,256]{1,0:T(8,128)(2,1)}, bf16[512,128]{1,0:T(8,128)(2,1)}) custom-call(bf16[1024,128]{1,0:T(8,128)(2,1)} %bitcast.16, s32[1,512]{1,0:T(1,128)} %get-tuple-element.44.slot_ref, s32[6,1024]{1,0:T(8,128)} %get-tuple-element.46.places_ref, s32[1,2048]{1,0:T(1,128)} %ident_ref.3, bf16[4,64,512]{2,1,0:T(8,128)(2,1)} %get-tuple-element.49.inputs_ref, ...), custom_call_target="tpu_custom_call" | custom-call | tf_op jit(solution)/shard_map/pallas_call | solution.py:527
  118.3 42.7 %shard_map.227 = (bf16[64,16,256]{2,1,0:T(8,128)(2,1)}, bf16[8,256,128]{2,1,0:T(8,128)(2,1)}) custom-call(bf16[64,16,256]{2,1,0:T(8,128)(2,1)} %bitcast.19, bf16[6,256,128]{2,1,0:T(8,128)(2,1)} %bitcast.23, bf16[2,256,128]{2,1,0:T(8,128)(2,1)} %bitcast.27), custom_call_target="tpu_custom_call" | custom-call | tf_op jit(solution)/shard_map/pallas_call | solution.py:527
  160.9 4.1 %shard_map.228 = (bf16[2048,64]{1,0:T(8,128)(2,1)}, f32[64,192]{1,0:T(8,128)}, f32[64,64]{1,0:T(8,128)}, f32[64,256]{1,0:T(8,128)}, f32[256,64]{1,0:T(8,128)}, /...) custom-call(bf16[1024,256]{1,0:T(8,128)(2,1)} %bitcast.20, ...), custom_call_target="tpu_custom_call" | custom-call | tf_op jit(solution)/shard_map/pallas_call | solution.py:527
  165.0 0.0 copy-start
  165.0 2.0 %copy.28 = bf16[1,2048,64]{1,2,0:T(8,128)(2,1)} copy(bf16[1,2048,64]{2,1,0:T(8,128)(2,1)} %bitcast.18) | data formatting | bytes 524288
  167.0 0.0 copy-done
  167.0 0.7 copy.29
Async XLA Ops:
  165.0 2.0 %copy-start = (f32[256,64]{1,0:T(8,128)S(1)}, f32[256,64]{1,0:T(8,128)}, u32[]{:S(2)}) copy-start(f32[256,64]{1,0:T(8,128)} %get-tuple-element.78) | copy-start | bytes 196612

commit v2 on v1

v2 whole, which is shorter than its diff:
```python
import math

import jax
import jax.numpy as jnp
from jax import lax
from jax.experimental import pallas as pl
from jax.experimental.pallas import tpu as pltpu
from jax.sharding import PartitionSpec as P


HEAD = 16
PATCH = 512
PATCHES = 4
ROWS = 2048
COARSE = 512
PEERS = 64
NEAR, FAR = 8, 32
MESH = pl.DeviceIdType.MESH
SHARPEN = HEAD**-0.5 / math.log(2.0)
f32, bf16, i32 = jnp.float32, jnp.bfloat16, jnp.int32


def dot(left, right):
    return jnp.dot(left, right, preferred_element_type=f32)


def dot_nt(left, right):
    return lax.dot_general(left, right, (((1,), (1,)), ((), ())), preferred_element_type=f32)


def turned(array):
    return array.astype(f32).T.astype(bf16)


def rows_of(count, width):
    return lax.broadcasted_iota(i32, (count, width), 0)


def match(row, count):
    return jnp.where(rows_of(count, row.shape[1]) == row, 1.0, 0.0).astype(bf16)


def norm(values):
    centred = values - jnp.mean(values, axis=0, keepdims=True)
    rate = lax.rsqrt(jnp.mean(centred * centred, axis=0, keepdims=True) + 1e-05)
    return centred * rate, rate


def norm_back(gradient, normed, rate):
    mean = jnp.mean(gradient, axis=0, keepdims=True)
    along = jnp.mean(gradient * normed, axis=0, keepdims=True)
    return rate * (gradient - mean - normed * along)


def padded(rows, head, width):
    parts = [rows]
    if head > 0:
        parts.insert(0, jnp.zeros((HEAD * head, rows.shape[1]), rows.dtype))
    rest = width - HEAD * (head + 1)
    if rest > 0:
        parts.append(jnp.zeros((rest, rows.shape[1]), rows.dtype))
    return jnp.concatenate(parts, axis=0)


def only(array, head):
    return padded(array[HEAD * head : HEAD * (head + 1)], head, array.shape[0])


def attend(mixed, width, powers_ref, first_power):
    keys = turned(mixed[width : 2 * width])
    ones = jnp.ones((HEAD, PATCH), bf16)
    outs, shares = [], []
    for head in range(width // HEAD):
        scores = dot(keys, only(mixed[:width], head))
        top = jnp.max(scores, axis=0, keepdims=True)
        powers = jnp.exp2((scores - top) * SHARPEN).astype(bf16)
        powers_ref[first_power + head] = powers
        start = 2 * width + HEAD * head
        sums = dot(jnp.concatenate([mixed[start : start + HEAD], ones], axis=0), powers)
        share = 1.0 / sums[HEAD : HEAD + 1]
        outs.append(sums[:HEAD] * share)
        shares.append(share)
    return jnp.concatenate(outs, axis=0).astype(bf16), jnp.concatenate(shares, axis=0)


def attend_back(mixed, attended, gradient, shares, width, powers_ref, first_power):
    keys = turned(mixed[width : 2 * width])
    values = turned(mixed[2 * width :])
    grad_queries, grad_keys, grad_values = [], [], []
    for head in range(width // HEAD):
        part = slice(HEAD * head, HEAD * (head + 1))
        queries = mixed[part]
        key_rows = mixed[width + HEAD * head : width + HEAD * (head + 1)]
        shared = gradient[part] * shares[head : head + 1]
        overlap = jnp.sum(shared * attended[part].astype(f32), axis=0, keepdims=True)
        shared = shared.astype(bf16)
        powers = powers_ref[first_power + head]
        spread = dot(values, padded(shared, head, width))
        change = (powers.astype(f32) * (spread - overlap)).astype(bf16)
        grad_queries.append(dot(key_rows, change) * HEAD**-0.5)
        grad_keys.append(dot_nt(queries, change) * HEAD**-0.5)
        grad_values.append(dot_nt(shared, powers))
    return jnp.concatenate(grad_queries + grad_keys + grad_values, axis=0).astype(bf16)


def block_front(inputs, inlet_t, outlet_t, widen_t, narrow_t, powers_ref, first_power):
    width = inputs.shape[0]
    start = inputs.astype(f32)
    normed = norm(start)[0].astype(bf16)
    mixed = dot(inlet_t, normed).astype(bf16)
    attended, shares = attend(mixed, width, powers_ref, first_power)
    middle = start + dot(outlet_t, attended)
    second = norm(middle)[0].astype(bf16)
    values = dot(widen_t, second)
    below = 0.5 + 0.5 * lax.erf(values * math.sqrt(0.5))
    hidden = (values * below).astype(bf16)
    result = (middle + dot(narrow_t, hidden)).astype(bf16)
    return result, mixed, attended, shares, hidden, values, below


def gelu_slope(values, below):
    bell = jnp.exp(-0.5 * values * values) * (1.0 / math.sqrt(2.0 * math.pi))
    return (below + values * bell).astype(bf16)


def block_back(inputs, mixed, attended, shares, hidden, slope, gradient, weights, outlet_t, powers_ref, first_power):
    inlet, outlet, widen, narrow = weights
    width = inputs.shape[0]
    start = inputs.astype(f32)
    normed, rate = norm(start)
    second, rate_two = norm(start + dot(outlet_t, attended))
    grad_wide = (dot(narrow, gradient) * slope.astype(f32)).astype(bf16)
    grad_middle = gradient.astype(f32) + norm_back(dot(widen, grad_wide), second, rate_two)
    short = grad_middle.astype(bf16)
    grad_mixed = attend_back(mixed, attended, dot(outlet, short), shares, width, powers_ref, first_power)
    grad_inputs = grad_middle + norm_back(dot(inlet, grad_mixed), normed, rate)

    def weight_grads():
        return (
            dot_nt(normed.astype(bf16), grad_mixed),
            dot_nt(attended, short),
            dot_nt(second.astype(bf16), grad_wide),
            dot_nt(gradient, hidden),
        )

    return grad_inputs.astype(bf16), weight_grads


def ranks(owner):
    before_me = jnp.where(rows_of(256, 256) < lax.broadcasted_iota(i32, (256, 256), 1), 1.0, 0.0)
    before_me = before_me.astype(bf16)
    before = jnp.zeros((PEERS, 1), f32)
    found = []
    for start in range(0, owner.shape[1], 256):
        hits = jnp.where(rows_of(PEERS, 256) == owner[:, start : start + 256], 1.0, 0.0)
        count = dot(hits.astype(bf16), before_me) + before
        found.append(jnp.sum(hits * count, axis=0, keepdims=True))
        before = before + jnp.sum(hits, axis=1, keepdims=True)
    return jnp.concatenate(found, axis=1).astype(i32)


def marks(owner, rank, value):
    hits = match(owner, PEERS)
    at = rows_of(128, owner.shape[1]) == rank
    high = jnp.where(at, (value >> 6).astype(f32), 0.0).astype(bf16)
    low = jnp.where(at, (value & 63).astype(f32), 0.0).astype(bf16)
    return dot_nt(hits, high) * 64.0 + dot_nt(hits, low)


def spread_places(table):
    lane = lax.broadcasted_iota(i32, (PEERS, 128), 1)
    apart = table + jnp.where(lane >= 64, 4096.0, 0.0)
    over = jnp.zeros((PEERS, 128), f32)
    for shift in range(1, 64):
        over = jnp.where(apart == pltpu.roll(apart, 128 - shift, 1), 1.0, over)
    high = jnp.floor(table * (1.0 / 64.0))
    low = table - 64.0 * high
    high = high + 64.0 * over
    stack = []
    for part in range(5):
        stack += [high[:, 16 * part : 16 * part + 16], low[:, 16 * part : 16 * part + 16]]
    stack = jnp.concatenate(stack, axis=0).astype(bf16)
    column = lax.broadcasted_iota(i32, (16, 1024), 1)
    spread = dot(stack, jnp.where(column % 16 == rows_of(16, 1024), 1.0, 0.0).astype(bf16))
    own = rows_of(PEERS, 1024) == lax.broadcasted_iota(i32, (PEERS, 1024), 1) // 16
    places, drops = [], []
    for part in range(5):
        high = jnp.sum(jnp.where(own, spread[128 * part : 128 * part + 64], 0.0), axis=0, keepdims=True)
        low = jnp.sum(jnp.where(own, spread[128 * part + 64 : 128 * part + 128], 0.0), axis=0, keepdims=True)
        drops.append(high > 63.5)
        high = jnp.where(high > 63.5, high - 64.0, high)
        places.append((high * 64.0 + low).astype(i32) - 1)
    return places, drops


def last_senders(inside, hits):
    width = hits[0].shape[0]
    count = len(inside[0])
    sender = lax.broadcasted_iota(i32, (1, 1024), 1) // 16
    own = rows_of(PEERS, 1024) == sender
    seen = jnp.zeros((PEERS * count, width), f32)
    for masks, hit in zip(inside, hits):
        wide = [jnp.where(own & mask, 1.0, 0.0) for mask in masks]
        seen += dot_nt(jnp.concatenate(wide, axis=0).astype(bf16), hit)
    index = rows_of(PEERS, width).astype(f32)
    lasts = []
    for part in range(count):
        lasts.append(jnp.max(jnp.where(seen[PEERS * part : PEERS * part + PEERS] > 0.5, index, -1.0), axis=0, keepdims=True))
    lasts = jnp.concatenate(lasts + [jnp.zeros((16 - count, width), f32)], axis=0).astype(bf16)
    found = []
    for masks, hit in zip(inside, hits):
        got = dot(lasts, hit)
        mine = jnp.full((1, 1024), -1.0, f32)
        for part in range(count):
            mine = jnp.where(masks[part], got[part : part + 1], mine)
        found.append(mine == sender.astype(f32))
    return found


def greet_peers(me):
    barrier = pltpu.get_barrier_semaphore()

    def greet(step, carry):
        pl.semaphore_signal(
            barrier, device_id={"pts": (me + step) % PEERS}, device_id_type=MESH
        )
        return carry

    lax.fori_loop(1, PEERS, greet, 0)
    return barrier


def send_to(source, target, sems, index, device):
    return pltpu.make_async_remote_copy(
        source, target, sems.at[index], sems.at[index + 1], device_id=device, device_id_type=MESH
    )


def batch_of(me, target, count, sems, index):
    some = target.at[pl.ds(0, count - 1)]
    return send_to(some, some, sems, index, {"pts": me})


def exchange(me, source, target, sems, index):

    def send(step, carry):
        other = (me + step) % PEERS
        send_to(source.at[other], target.at[me], sems, index, {"pts": other}).start()
        return carry

    lax.fori_loop(1, PEERS, send, 0)
    target[me] = source[me]
    return batch_of(me, target, PEERS, sems, index)


def exchange_parts(me, make_part, source, target, sems, index):
    for turn in range(4):
        quarter = (me // 16 + turn) % 4
        source[pl.ds(16 * quarter, 16)] = make_part(quarter)

        def send(step, carry, quarter=quarter):
            other = 16 * quarter + (me + step) % 16
            send_to(source.at[other], target.at[me], sems, index, {"pts": other}).start()
            return carry

        lax.fori_loop(1 if turn == 0 else 0, 16, send, 0)
    target[me] = source[me]
    return batch_of(me, target, PEERS, sems, index)


class Adder:
    def __init__(self, scale, half, near, middle, far, chunk, whole, flat, near_out, out, sems, index):
        self.scale, self.half, self.near, self.middle, self.far = scale, half, near, middle, far
        self.chunk, self.whole, self.flat, self.near_out, self.out = chunk, whole, flat, near_out, out
        self.sems, self.index, self.unit = sems, index, chunk.shape[0]
        self.me, rep = lax.axis_index("pts"), lax.axis_index("rep")
        self.place, self.core = self.me // 2, self.me % 2
        self.mine = self.core * 4 + rep

    def near_device(self, step):
        other = (self.mine + step) % NEAR
        return other, {"pts": self.place * 2 + other // 4, "rep": other % 4}

    def far_device(self, step):
        other = (self.place + step) % FAR
        return other, {"pts": other * 2 + self.core}

    def batch(self, target, count, stage):
        return batch_of(self.me, target, count, self.sems, self.index + 2 * stage)

    def loop(self, count, source, target, stage, device_of):
        def send(step, carry):
            other, device = device_of(step)
            block = source.at[other] if source.shape[0] == count and len(source.shape) == 3 else source
            send_to(block, target, self.sems, self.index + 2 * stage, device).start()
            return carry

        lax.fori_loop(1, count, send, 0)

    def send_near(self):
        self.loop(NEAR, self.half, self.near.at[self.mine], 0, self.near_device)
        self.near[self.mine] = self.half[self.mine]

    def send_far(self):
        self.batch(self.near, NEAR, 0).wait_recv()
        total = self.near[0].astype(f32)
        for index in range(1, NEAR):
            total = total + self.near[index].astype(f32)
        for index in range(FAR):
            self.middle[index] = total[self.unit * index : self.unit * (index + 1)]
        self.loop(FAR, self.middle, self.far.at[self.place], 1, self.far_device)
        self.far[self.place] = self.middle[self.place]

    def spread_far(self):
        self.batch(self.far, FAR, 1).wait_recv()
        self.chunk[...] = jnp.sum(self.far[...], axis=0) * self.scale
        self.loop(FAR, self.chunk, self.whole.at[self.place], 2, self.far_device)
        self.whole[self.place] = self.chunk[...]

    def spread_near(self):
        self.batch(self.whole, FAR, 2).wait_recv()
        for index in range(FAR):
            self.flat[self.unit * index : self.unit * (index + 1), :] = self.whole[index]
        self.near_out[...] = self.flat[...].astype(bf16)
        self.loop(NEAR, self.near_out, self.out.at[self.mine], 3, self.near_device)
        self.out[self.mine] = self.near_out[...]

    def end(self):
        self.batch(self.out, NEAR, 3).wait_recv()
        self.batch(self.near, NEAR, 0).wait_send()
        self.batch(self.far, FAR, 1).wait_send()
        self.batch(self.whole, FAR, 2).wait_send()
        self.batch(self.out, NEAR, 3).wait_send()


def adder_scratch(rows):
    unit = rows // FAR
    return [
        pltpu.VMEM((NEAR, rows, 128), bf16),
        pltpu.VMEM((NEAR, rows, 128), bf16),
        pltpu.VMEM((FAR, unit, 128), f32),
        pltpu.VMEM((FAR, unit, 128), f32),
        pltpu.VMEM((unit, 128), f32),
        pltpu.VMEM((FAR, unit, 128), f32),
        pltpu.VMEM((rows, 128), f32),
        pltpu.VMEM((rows, 128), bf16),
    ]


def store_lanes(ref, row, array):
    height, block = array.shape[0], ref.shape[1]
    for index in range(array.shape[1] // 128):
        part = array[:, 128 * index : 128 * index + 128].astype(ref.dtype)
        start, done = row + height * index, 0
        while done < height:
            count = min(height - done, block - (start + done) % block)
            inside = (start + done) % block
            ref[(start + done) // block, inside : inside + count, :] = part[done : done + count]
            done += count


def load_lanes(ref, row, height, count):
    parts = [ref[row + height * index : row + height * (index + 1), :].astype(f32) for index in range(count)]
    return jnp.concatenate(parts, axis=1) if count > 1 else parts[0]


def main_kernel(
    scale,
    feats_ref, first_ref, ident_ref, second_ref, cotangent_ref,
    inlet_one, outlet_one, widen_one, narrow_one_t, pool_ref, inlet_two, outlet_two, widen_two, narrow_two,
    second_out, feats_out, sums_one, sums_two,
    mark, marks_in, send_one, rows_one, send_two, rows_two, send_three, rows_three, send_four, rows_four,
    places_ref, inputs_ref, mixed_ref, attended_ref, shares_ref, hidden_ref, values_ref, below_ref, slope_ref,
    powers_one, powers_two, total_ref, back_ref, front_total, widen_total, narrow_total, *rest,
):
    me = lax.axis_index("pts")
    sems = rest[-1]
    late = Adder(scale, *rest[:8], sums_one, sems, 10)
    early = Adder(scale, *rest[8:16], sums_two, sems, 18)
    barrier = greet_peers(me)

    def greet_near(step, carry):
        pl.semaphore_signal(barrier, device_id=early.near_device(step)[1], device_id_type=MESH)
        return carry

    lax.fori_loop(1, NEAR, greet_near, 0)

    first, second = first_ref[...], second_ref[...]
    owner_one, owner_two = first // ROWS, second // COARSE
    rank_one, rank_two = ranks(owner_one), ranks(owner_two)
    found = marks(owner_one, rank_one, first % ROWS + 1)
    found += marks(owner_two, rank_two + 64, second % COARSE + 1)
    mark[:, 0, :] = found
    slot_one, layer_one = owner_one * 16 + rank_one % 16, rank_one // 16
    slot_two = owner_two * 16 + rank_two
    feats = feats_ref[...].astype(f32)
    wide = [jnp.where(layer_one == index, feats, 0.0) for index in range(4)]
    wide = jnp.concatenate(wide, axis=0).astype(bf16)
    pl.semaphore_wait(barrier, PEERS + NEAR - 2)
    marked = exchange(me, mark, marks_in, sems, 0)

    def pack(quarter):
        return dot_nt(match(slot_one - 256 * quarter, 256), wide).astype(bf16).reshape(16, 16, 256)

    moved_one = exchange_parts(me, pack, send_one, rows_one, sems, 2)

    marked.wait_recv()
    places, drops = spread_places(marks_in[:, 0, :])
    for part in range(5):
        places_ref[part : part + 1, :] = places[part]
    kept = [jnp.where(drop, -1, place) for place, drop in zip(places, drops)]
    hits = [match(place % 512, 512) for place in kept[:4]]
    last = last_senders([[place // 512 == patch for patch in range(PATCHES)] for place in kept[:4]], hits)
    last_two = last_senders([[kept[4] >= 0]], [match(kept[4], COARSE)])
    places_ref[5:6, :] = jnp.where(last_two[0], kept[4], -1)
    weights_one = [inlet_one[...], outlet_one[...], widen_one[...], turned(narrow_one_t[...])]
    turned_one = [turned(weight) for weight in weights_one[:3]] + [narrow_one_t[...]]

    moved_one.wait_recv()
    arrived = rows_one[...].reshape(1024, 256).astype(f32).T
    landed = jnp.zeros((256, 512), f32)
    for layer in range(4):
        place = jnp.where(last[layer], kept[layer], -1)
        points = arrived[64 * layer : 64 * layer + 64]
        spread = [jnp.where(place // 512 == patch, points, 0.0) for patch in range(PATCHES)]
        landed += dot_nt(jnp.concatenate(spread, axis=0).astype(bf16), hits[layer])
    inputs_ref[...] = landed.astype(bf16).reshape(PATCHES, 64, PATCH)
    total_ref[...] = jnp.zeros_like(total_ref)

    def ident_of(patch):
        return ident_ref[:, pl.ds(pl.multiple_of(patch * PATCH, PATCH), PATCH)]

    def front(patch, carry):
        result, mixed, attended, shares, hidden, values, below = block_front(
            inputs_ref[patch], *turned_one, powers_one, 4 * patch
        )
        mixed_ref[patch] = mixed
        attended_ref[patch] = attended
        shares_ref[patch] = shares
        hidden_ref[patch] = hidden
        values_ref[patch] = values
        below_ref[patch] = below
        counted = jnp.concatenate([result, jnp.ones((16, PATCH), bf16)], axis=0)
        total_ref[...] += dot_nt(counted, match(ident_of(patch), COARSE))
        return carry

    lax.fori_loop(0, PATCHES, front, 0)
    sizes = total_ref[64:65]
    pooled = (total_ref[:64] / sizes).astype(bf16)
    coarse = dot(turned(pool_ref[...]), pooled).astype(bf16)
    send_two[...] = dot_nt(match(slot_two, 1024), coarse).astype(bf16).reshape(PEERS, 16, 128)
    moved_two = exchange(me, send_two, rows_two, sems, 4)

    def slopes(patch, carry):
        slope_ref[patch] = gelu_slope(values_ref[patch], below_ref[patch])
        return carry

    lax.fori_loop(0, PATCHES, slopes, 0)
    weights_two = [inlet_two[...], outlet_two[...], widen_two[...], narrow_two[...]]
    turned_two = [turned(weight) for weight in weights_two]
    gradient = turned(cotangent_ref[...])
    landing = match(places_ref[5:6, :], COARSE)
    moved_two.wait_recv()

    inputs = dot_nt(turned(rows_two[...].reshape(1024, 128)), landing).astype(bf16)
    result, mixed, attended, shares, hidden, values, below = block_front(inputs, *turned_two, powers_two, 0)
    back, grads_of = block_back(
        inputs, mixed, attended, shares, hidden, gelu_slope(values, below), gradient,
        weights_two, turned_two[1], powers_two, 0,
    )
    send_three[...] = turned(dot(back, match(places_ref[4:5, :], COARSE))).reshape(PEERS, 16, 128)
    moved_three = exchange(me, send_three, rows_three, sems, 6)
    row = 0
    for grad in grads_of():
        store_lanes(early.half, row, grad)
        row += grad.shape[0] * grad.shape[1] // 128
    early.half[6:] = jnp.zeros((2, 256, 128), bf16)
    early.send_near()
    second_out[...] = turned(result)
    front_total[...] = jnp.zeros_like(front_total)
    widen_total[...] = jnp.zeros_like(widen_total)
    narrow_total[...] = jnp.zeros_like(narrow_total)
    taking = match(slot_two, 1024)
    moved_three.wait_recv()

    grad_coarse = dot(turned(rows_three[...].reshape(1024, 128)), taking).astype(bf16)
    grad_pool = dot_nt(pooled, grad_coarse)
    grad_pooled = dot(pool_ref[...], grad_coarse).astype(bf16).astype(f32)
    share = (grad_pooled / sizes).astype(bf16)

    def rear(patch, carry):
        gradient = dot(share, match(ident_of(patch), COARSE)).astype(bf16)
        back, grads_of = block_back(
            inputs_ref[patch], mixed_ref[patch], attended_ref[patch], shares_ref[patch], hidden_ref[patch],
            slope_ref[patch], gradient, weights_one, turned_one[1], powers_one, 4 * patch,
        )
        back_ref[patch] = back
        grad_inlet, grad_outlet, grad_widen, grad_narrow = grads_of()
        front_total[...] += jnp.concatenate([grad_inlet, grad_outlet], axis=1)
        widen_total[...] += grad_widen
        narrow_total[...] += grad_narrow
        pl.when(patch == 0)(early.send_far)
        pl.when(patch == 1)(early.spread_far)
        pl.when(patch == 2)(early.spread_near)
        return carry

    lax.fori_loop(0, PATCHES, rear, 0)
    store_lanes(late.half, 0, front_total[...])
    store_lanes(late.half, 128, widen_total[...])
    store_lanes(late.half, 256, narrow_total[...])
    store_lanes(late.half, 384, grad_pool)
    late.half[7] = jnp.zeros((64, 128), bf16)
    late.send_near()
    back = back_ref[...].reshape(256, PATCH)

    def take(quarter):
        taken = []
        for layer in range(4):
            place = places_ref[layer : layer + 1, pl.ds(pl.multiple_of(quarter * 256, 256), 256)]
            found = dot(back, match(place % 512, 512))
            parts = [
                jnp.where(place // 512 == patch, found[64 * patch : 64 * patch + 64], 0.0) for patch in range(PATCHES)
            ]
            taken.append(parts[0] + parts[1] + parts[2] + parts[3])
        return jnp.concatenate(taken, axis=0).T.astype(bf16).reshape(16, 16, 256)

    moved_four = exchange_parts(me, take, send_four, rows_four, sems, 8)
    late.send_far()
    picking = match(slot_one, 1024)
    late.spread_far()
    late.spread_near()
    moved_four.wait_recv()
    found = dot(turned(rows_four[...].reshape(1024, 256)), picking)
    parts = [jnp.where(layer_one == index, found[64 * index : 64 * index + 64], 0.0) for index in range(4)]
    feats_out[...] = (parts[0] + parts[1] + parts[2] + parts[3]).astype(bf16)
    early.end()
    late.end()
    marked.wait_send()
    moved_one.wait_send()
    moved_two.wait_send()
    moved_three.wait_send()
    moved_four.wait_send()


def output_kernel(
    second_in, feats_in, late_ref, early_ref,
    second_out, feats_out, inlet_one, outlet_one, widen_one, narrow_one_t, pool,
    inlet_two, outlet_two, widen_two, narrow_two,
):
    second_out[...] = second_in[...]
    feats_out[...] = feats_in[...]
    front = load_lanes(late_ref, 0, 64, 2)
    inlet_one[...] = front[:, :192]
    outlet_one[...] = front[:, 192:]
    widen_one[...] = load_lanes(late_ref, 128, 64, 2)
    narrow_one_t[...] = load_lanes(late_ref, 256, 64, 2)
    pool[...] = load_lanes(late_ref, 384, 64, 1)
    inlet_two[...] = load_lanes(early_ref, 0, 128, 3)
    outlet_two[...] = load_lanes(early_ref, 384, 128, 1)
    widen_two[...] = load_lanes(early_ref, 512, 128, 4)
    narrow_two[...] = load_lanes(early_ref, 1024, 128, 4).T


def call(kernel, outs, scratch, *operands, collective=None):
    params = {} if collective is None else {"collective_id": collective, "has_side_effects": True}
    whole = pl.BlockSpec(memory_space=pltpu.VMEM)
    return pl.pallas_call(
        kernel,
        out_shape=[jax.ShapeDtypeStruct(shape, dtype) for shape, dtype in outs],
        in_specs=[whole] * len(operands),
        out_specs=[whole] * len(outs),
        scratch_shapes=scratch,
        compiler_params=pltpu.CompilerParams(vmem_limit_bytes=56 * 2**20, **params),
    )(*operands)


def shards(
    feats,
    dest_first,
    pool_ids,
    dest_second,
    cotangent,
    inlet_first,
    outlet_first,
    widen_first,
    narrow_first,
    pool_weight,
    inlet_second,
    outlet_second,
    widen_second,
    narrow_second,
):
    scale = 1.0 / math.sqrt(lax.axis_size("rep") * lax.axis_size("pts") * COARSE)
    wide_slots, slots = pltpu.VMEM((PEERS, 16, 256), bf16), pltpu.VMEM((PEERS, 16, 128), bf16)
    mark = pltpu.VMEM((PEERS, 1, 128), f32)
    moved = call(
        lambda *refs: main_kernel(scale, *refs),
        [((COARSE, 128), bf16), ((64, ROWS), bf16), ((NEAR, 64, 128), bf16), ((NEAR, 256, 128), bf16)],
        [mark, mark, wide_slots, wide_slots, slots, slots, slots, slots, wide_slots, wide_slots]
        + [
            pltpu.VMEM((6, 1024), i32),
            pltpu.VMEM((PATCHES, 64, PATCH), bf16),
            pltpu.VMEM((PATCHES, 192, PATCH), bf16),
            pltpu.VMEM((PATCHES, 64, PATCH), bf16),
            pltpu.VMEM((PATCHES, 4, PATCH), f32),
            pltpu.VMEM((PATCHES, 256, PATCH), bf16),
            pltpu.VMEM((PATCHES, 256, PATCH), f32),
            pltpu.VMEM((PATCHES, 256, PATCH), f32),
            pltpu.VMEM((PATCHES, 256, PATCH), bf16),
            pltpu.VMEM((16, PATCH, PATCH), bf16),
            pltpu.VMEM((8, PATCH, PATCH), bf16),
            pltpu.VMEM((80, COARSE), f32),
            pltpu.VMEM((PATCHES, 64, PATCH), bf16),
            pltpu.VMEM((64, 256), f32),
            pltpu.VMEM((64, 256), f32),
            pltpu.VMEM((64, 256), f32),
        ]
        + adder_scratch(64)
        + adder_scratch(256)
        + [pltpu.SemaphoreType.DMA((26,))],
        feats[0].T, dest_first, pool_ids, dest_second, cotangent[0],
        inlet_first, outlet_first, widen_first, narrow_first.T, pool_weight,
        inlet_second, outlet_second, widen_second, narrow_second,
        collective=1,
    )
    second_out, feats_grad, late, early = moved
    weights = (inlet_first, outlet_first, widen_first, narrow_first.T, pool_weight)
    weights += (inlet_second, outlet_second, widen_second, narrow_second)
    second_out, feats_grad, *totals = call(
        output_kernel,
        [((COARSE, 128), bf16), ((64, ROWS), bf16)] + [(weight.shape, f32) for weight in weights],
        [],
        second_out, feats_grad, late.reshape(512, 128), early.reshape(2048, 128),
    )
    totals[3] = totals[3].T
    return (second_out[None], feats_grad.T[None], *totals)


def solution(mesh):
    split = P("rep", "pts")
    return jax.shard_map(
        shards,
        mesh=mesh,
        in_specs=(split,) * 5 + (P(),) * 9,
        out_specs=(split,) * 2 + (P(),) * 9,
        check_vma=False,
    )
```

time: 168 us -> 130 us (0.77)
  Pallas kernels: 161 us -> 128 us
  local copies, waits for them, and re-layouts: 6.13 us -> 0 us
    pallas_call x8 -> x2, Pallas kernels: 161 us -> 128 us  [call(): pl.pallas_call(kernel, out_shape=[jax.ShapeDtypeStruct(shape, dtype) for...]
    unnamed x6 -> x0, local copies, waits for them, and re-layouts: 6.13 us -> none
where the time goes in v2:
time: 130 us; the launch traced here: 128 us
  Pallas kernels  128 us (98%)
    pallas_call x2, Pallas kernels, call(): pl.pallas_call(kernel, out_shape=[jax.ShapeDtypeStruct(shape, dtype) for...  128 us

profile of v2, /device:TPU:32, one launch (start us, length us, event | category | flops | bytes accessed | tf_op | source)
XLA Modules:
  0.0 128.4 jit_solution(3069686035959336582)
XLA Ops:
  0.6 125.3 %shard_map.221 = (bf16[512,128]{1,0:T(8,128)(2,1)}, bf16[64,2048]{1,0:T(8,128)(2,1)}, bf16[8,64,128]{2,1,0:T(8,128)(2,1)}, bf16[8,256,128]{2,1,0:T(8,128)(2,1)}) custom-call(bf16[64,2048]{1,0:T(8,128)(2,1)} %bitcast.13, s32[1,2048]{1,0:T(1,128)} %refs_1_.1, s32[1,2048]{1,0:T(1,128)} %refs_2_.1, s32[1,512]{1,0:T(1,128)} %refs_3_.1, ...), custom_call_target="tpu_custom_call" | custom-call | tf_op jit(solution)/shard_map/pallas_call | solution.py:567
  126.0 2.4 %shard_map.222 = (bf16[512,128]{1,0:T(8,128)(2,1)}, bf16[64,2048]{1,0:T(8,128)(2,1)}, f32[64,192]{1,0:T(8,128)}, f32[64,64]{1,0:T(8,128)}, f32[64,256]{1,0:T(8,1...) custom-call(bf16[512,128]{1,0:T(8,128)(2,1)} %get-tuple-element.26.s, ...), custom_call_target="tpu_custom_call" | custom-call | tf_op jit(solution)/shard_map/pallas_call | solution.py:567
